TPU v7x, 512 devices: a whole 4x8x8 slice. The times are simulated.
512 devices in a mesh: row: 32 (over x, y), col: 16 (over z, core).
Axes of the slice: x: 4, y: 8, z: 8, core: 2. Of those that a mesh axis runs over, the one named last changes fastest.
Arguments:
- embeddings: float32 [64, 32768], P(None, 'col'), may hold values from -0.75 to 0.75
- confidence: bfloat16 [32768, 32768], P('row', 'col'), may hold values from 0.049804688 to 1
- sketch: float32 [40, 32768], P(None, 'col'), may hold values from -6 to 6
Outputs:
- basis: float32 [40, 32768], P(None, 'row')
- r_factor: float32 [40, 40], replicated
All inputs are finite; a program needn't handle non-finite values.
Results may differ from a plain program's by a relative error of at most 0.0003.
Values sent between devices are 32-bit elements; how exact they have to be, the bound alone decides.
No kernel may reach another device: no remote copies, remote signals or barrier semaphores. Data moves between devices by JAX's collectives and lax.ppermute only.
A program may use at most 64 MiB of HBM per device.

v0:
```python
import math

import jax
import jax.numpy as jnp
from jax import lax
from jax.sharding import PartitionSpec as P

HIGHEST_PRECISION = lax.Precision.HIGHEST


def contract_last(left, right):
    return lax.dot_general(
        left,
        right,
        (((1,), (1,)), ((), ())),
        precision=HIGHEST_PRECISION,
        preferred_element_type=jnp.float32,
    )


def cholesky_pass(gram_matrix, block_rows):
    factor_low = jnp.linalg.cholesky(gram_matrix)
    solved = lax.linalg.triangular_solve(factor_low, block_rows, left_side=True, lower=True)
    return (solved, factor_low.T)


def gram_total(block_rows):
    return lax.psum(contract_last(block_rows, block_rows), "row")


def local(embeddings, confidence, sketch):
    rows_axis = lax.axis_size("row")
    row_dev = confidence.shape[0]
    count_all = row_dev * rows_axis
    rindex = lax.axis_index("row")
    gathered = lax.all_gather(embeddings, "col", axis=1, tiled=True)
    points = lax.dynamic_slice_in_dim(gathered, rindex * row_dev, row_dev, 1)
    norms_col = jnp.sum(embeddings * embeddings, axis=0)
    norms_row = jnp.sum(points * points, axis=0)
    inner_prod = lax.dot_general(
        points,
        embeddings,
        (((0,), (0,)), ((), ())),
        precision=HIGHEST_PRECISION,
        preferred_element_type=jnp.float32,
    )
    distance = norms_row[:, None] + norms_col[None, :] - 2.0 * inner_prod
    weighted = confidence.astype(jnp.float32) * distance
    totals = lax.psum(jnp.sum(sketch, axis=1), "col")
    centred = sketch - (totals / count_all)[:, None]
    product = lax.psum(contract_last(centred, weighted), "col")
    row_mean = lax.psum(jnp.sum(product, axis=1), "row") / count_all
    lowered = -0.5 * (product - row_mean[:, None])
    basis_one, upper_one = cholesky_pass(gram_total(lowered), lowered)
    basis_two, upper_two = cholesky_pass(gram_total(basis_one), basis_one)
    upper_tri = jnp.dot(upper_two, upper_one, precision=HIGHEST_PRECISION)
    basis = math.sqrt(count_all) * basis_two
    return (basis, upper_tri / count_all)


def solution(mesh):
    placed = (P(None, "col"), P("row", "col"), P(None, "col"))
    return jax.shard_map(
        local, mesh=mesh, in_specs=placed, out_specs=(P(None, "row"), P()), check_vma=False
    )
```

profile of v0, /device:TPU:64, one launch (start us, length us, event | category | flops | bytes accessed | tf_op | source)
XLA Modules:
  0.0 578.1 jit_solution(17494467870442178313)
XLA Ops:
  7.2 0.0 copy-start.1
  7.2 0.0 all-gather.2.cloned.1.call-start
  7.2 0.7 all-gather.2.cloned.1.call-update
  7.9 0.0 all-reduce.2.cloned.1.call-start
  8.0 1.1 reduce_sum.36
  9.1 28.7 %psum.35 = f32[40]{0:T(128)S(1)} all-reduce(f32[40]{0:T(128)S(1)} %reduce_sum.36), channel_id=1, replica_groups=mesh['row'=32,'col'=16] {'col'}, use_global_device_ids=true, to_apply=%region_1.0 | all-reduce | flops 40 | bytes 320 | tf_op jit(solution)/shard_map/psum | solution.py:49
  37.7 1.1 multiply_reduce_fusion
  38.9 32.3 %all-gather.2.cloned.1.call-done = f32[64,32768]{1,0:T(8,128)} async-done(((f32[64,2048]{1,0:T(8,128)}), f32[64,32768]{1,0:T(8,128)}) %all-gather.2.cloned.1.call-update) | async-done | bytes 8388624 | tf_op jit(solution)/shard_map/all_gather | solution.py:36
  71.2 0.0 copy-start
  71.2 8.2 %fusion.10 = f32[1024,2048]{1,0:T(8,128)S(1)} fusion(f32[64,2048]{1,0:T(8,128)} %param.6, f32[64,32768]{1,0:T(8,128)} %all-gather.2.cloned.1.call-done, s32[]{:T(128)S(6)} %select_n.6), kind=kOutput, calls=%fused_computation.14 | convolution fusion | flops 1610612736 | bytes 9175044 | tf_op jit(solution)/shard_map/dot_general | solution.py:40
  79.3 1.0 multiply_reduce_fusion.1
  80.3 0.0 copy-done.1
  80.3 0.0 copy-done
  80.3 9.3 %fusion = f32[40,1024]{1,0:T(8,128)} fusion(f32[1024,2048]{1,0:T(8,128)S(1)} %fusion.10, bf16[1024,2048]{1,0:T(8,128)(2,1)S(1)} %copy-done, f32[2048]{0:T(1024)S(1)} %multiply_reduce_fusion, f32[1024]{0:T(1024)S(1)} %multiply_reduce_fusion.1, f32[40,2048]{1,0:T(8,128)S(1)} %copy-done.1, f32[40]{0:T(128)S(1)} %broadcast_multiply_fusion.1), kind=kOutput, calls=%fused_computation | convolution fusion | flops 1017200640 | bytes 13086880 | tf_op jit(solution)/shard_map/dot_general | solution.py:12
  89.7 0.0 all-reduce.2.cloned.1.call-update
  89.7 108.1 %all-reduce.2.cloned.1.call-done = f32[40,1024]{1,0:T(8,128)} async-done(((f32[40,1024]{1,0:T(8,128)}), f32[40,1024]{1,0:T(8,128)}) %all-reduce.2.cloned.1.call-update) | async-done | bytes 163856 | tf_op jit(solution)/shard_map/psum | solution.py:51
  197.8 1.0 reduce_sum.39
  198.8 74.6 %psum.37 = f32[40]{0:T(128)S(1)} all-reduce(f32[40]{0:T(128)S(1)} %reduce_sum.39), channel_id=1, replica_groups=mesh['row'=32,'col'=16] {'row'}, use_global_device_ids=true, to_apply=%region_6.0 | all-reduce | flops 40 | bytes 320 | tf_op jit(solution)/shard_map/psum | solution.py:52
  273.4 1.3 fusion.14
  274.8 137.7 %psum.38 = f32[40,40]{0,1:T(8,128)S(1)} all-reduce(f32[40,40]{0,1:T(8,128)S(1)} %fusion.14), channel_id=1, replica_groups=mesh['row'=32,'col'=16] {'row'}, use_global_device_ids=true, to_apply=%region_7.0 | all-reduce | flops 1600 | bytes 12800 | tf_op jit(solution)/shard_map/psum | solution.py:28
  412.4 0.1 copy.6
  412.5 3.6 cholesky.44
  416.2 0.6 compare_reduce_fusion.1
  416.9 0.7 fusion.26
  417.5 3.1 custom-call.6
  420.6 1.3 fusion.13
  421.9 0.3 fusion.41
  422.2 137.7 %psum.39 = f32[40,40]{0,1:T(8,128)S(1)} all-reduce(f32[40,40]{0,1:T(8,128)S(1)} %fusion.41), channel_id=1, replica_groups=mesh['row'=32,'col'=16] {'row'}, use_global_device_ids=true, to_apply=%region_10.13 | all-reduce | flops 1600 | bytes 12800 | tf_op jit(solution)/shard_map/psum | solution.py:28
  559.8 0.1 copy.8
  559.9 3.6 cholesky.55
  563.6 0.7 compare_reduce_fusion
  564.3 2.2 convolution_multiply_fusion.1
  566.5 0.7 select_bitcast_fusion
  567.2 3.1 custom-call.7
  570.3 1.0 convolution_multiply_fusion
  (6 shorter events, 0.1 us)
Async XLA Ops:
  7.2 73.2 %copy-start.1 = (f32[40,2048]{1,0:T(8,128)S(1)}, f32[40,2048]{1,0:T(8,128)}, u32[]{:S(2)}) copy-start(f32[40,2048]{1,0:T(8,128)} %param.8) | copy-start | bytes 983044
  7.2 64.0 %all-gather.2.cloned.1.call-start = ((), (), s32[]{:S(2)}) async-start(), calls=%async_computation | async-start | bytes 8912896 | tf_op jit(solution)/shard_map/all_gather | solution.py:36
  7.9 189.9 %all-reduce.2.cloned.1.call-start = ((), (), s32[]{:S(2)}) async-start(), calls=%async_computation.1 | async-start | bytes 327680 | tf_op jit(solution)/shard_map/psum | solution.py:51
  71.2 9.2 %copy-start = (bf16[1024,2048]{1,0:T(8,128)(2,1)S(1)}, bf16[1024,2048]{1,0:T(8,128)(2,1)}, u32[]{:S(2)}) copy-start(bf16[1024,2048]{1,0:T(8,128)(2,1)} %param.7) | copy-start | bytes 12582916
Sparse Core Ops, SparseCore 0:
  10.1 60.9 all-gather.1
  89.8 107.9 all-reduce.1
where the time goes:
time: 579 us; the launch traced here: 578 us
  blocking collectives  379 us (65%)
  waiting for transfers between devices  141 us (24%)
  matrix products  23.6 us (4%)
  other arithmetic  20.5 us (4%)
  between operations  14.1 us (2%)
    psum x2, blocking collectives, gram_total(): return lax.psum(contract_last(block_rows, block_rows), 'row')  275 us
    psum x1, waiting for transfers between devices, local(): product = lax.psum(contract_last(centred, weighted), 'col')  108 us
    psum x1, blocking collectives, local(): row_mean = lax.psum(jnp.sum(product, axis=1), 'row') / count_all  74.6 us
    all_gather x1, waiting for transfers between devices, local(): gathered = lax.all_gather(embeddings, 'col', axis=1, tiled=True)  32.3 us
    psum x1, blocking collectives, local(): totals = lax.psum(jnp.sum(sketch, axis=1), 'col')  28.7 us
  transfers between devices with their start and end apart: 2, of which 2 were waited for; matrix products, arithmetic and copies ran while one was open for 0% of the time, Pallas kernels for 0%

commit v1 on v0

--- a/solution.py
+++ b/solution.py
@@ -24,17 +24,42 @@
     return (solved, factor_low.T)
 
 
-def gram_total(block_rows):
-    return lax.psum(contract_last(block_rows, block_rows), "row")
+def exchange(blocks, axis):
+    return lax.all_to_all(blocks, axis, split_axis=0, concat_axis=0, tiled=True)
+
+
+def share(block, axis):
+    return exchange(jnp.broadcast_to(block[None], (lax.axis_size(axis),) + block.shape), axis)
+
+
+def doubling_sum(block, axis):
+    size = lax.axis_size(axis)
+    step = 1
+    while step < size:
+        block = block + lax.ppermute(block, axis, [(i, i ^ step) for i in range(size)])
+        step *= 2
+    return block
 
 
 def local(embeddings, confidence, sketch):
-    rows_axis = lax.axis_size("row")
-    row_dev = confidence.shape[0]
-    count_all = row_dev * rows_axis
+    n_row, n_col = lax.axis_size("row"), lax.axis_size("col")
+    row_dev, col_dev = confidence.shape
+    count_all = row_dev * n_row
+    halves = col_dev // row_dev
+    piece = row_dev // n_col
+    k = sketch.shape[0]
     rindex = lax.axis_index("row")
-    gathered = lax.all_gather(embeddings, "col", axis=1, tiled=True)
-    points = lax.dynamic_slice_in_dim(gathered, rindex * row_dev, row_dev, 1)
+
+    half = lax.dynamic_slice_in_dim(embeddings, (rindex % halves) * row_dev, row_dev, 1)
+    mine = lax.dynamic_slice_in_dim(half, (rindex // halves) * piece, piece, 1)
+    pairs = [
+        (r * n_col + c, (c * halves + r % halves) * n_col + r // halves)
+        for r in range(n_row)
+        for c in range(n_col)
+    ]
+    piece_points = lax.ppermute(mine, ("row", "col"), pairs)
+    points = jnp.transpose(share(piece_points, "col"), (1, 0, 2)).reshape(-1, row_dev)
+
     norms_col = jnp.sum(embeddings * embeddings, axis=0)
     norms_row = jnp.sum(points * points, axis=0)
     inner_prod = lax.dot_general(
@@ -46,13 +71,33 @@
     )
     distance = norms_row[:, None] + norms_col[None, :] - 2.0 * inner_prod
     weighted = confidence.astype(jnp.float32) * distance
-    totals = lax.psum(jnp.sum(sketch, axis=1), "col")
-    centred = sketch - (totals / count_all)[:, None]
-    product = lax.psum(contract_last(centred, weighted), "col")
-    row_mean = lax.psum(jnp.sum(product, axis=1), "row") / count_all
+
+    mean_here = jnp.sum(sketch, axis=1) / col_dev
+    centred = sketch - mean_here[:, None]
+    part = contract_last(jnp.concatenate([centred, jnp.ones((1, col_dev), jnp.float32)], 0), weighted)
+    cut = jnp.transpose(part.reshape(k + 1, n_col, piece), (1, 0, 2))
+    means = jnp.broadcast_to(jnp.pad(mean_here, (0, piece - k))[None, None, :], (n_col, 1, piece))
+    got = exchange(jnp.concatenate([cut, means], axis=1), "col")
+    mean_blocks = got[:, k + 1, :k]
+    shift = mean_blocks - jnp.sum(mean_blocks, axis=0) / n_col
+    product_piece = jnp.sum(got[:, :k] + shift[:, :, None] * got[:, k : k + 1], axis=0)
+    product = jnp.transpose(share(product_piece, "col"), (1, 0, 2)).reshape(k, row_dev)
+
+    mean_rows = jnp.sum(product, axis=1, keepdims=True) / row_dev
+    from_mean = product - mean_rows
+    gram = contract_last(from_mean, from_mean)
+    all_rows = share(jnp.concatenate([gram, mean_rows.T], axis=0), "row")
+    row_means = all_rows[:, k]
+    row_mean = jnp.sum(row_means, axis=0) / n_row
+    off = row_means - row_mean
+    between = lax.dot_general(
+        off, off, (((0,), (0,)), ((), ())), precision=HIGHEST_PRECISION, preferred_element_type=jnp.float32
+    )
+    gram_all = 0.25 * (jnp.sum(all_rows[:, :k], axis=0) + row_dev * between)
     lowered = -0.5 * (product - row_mean[:, None])
-    basis_one, upper_one = cholesky_pass(gram_total(lowered), lowered)
-    basis_two, upper_two = cholesky_pass(gram_total(basis_one), basis_one)
+    basis_one, upper_one = cholesky_pass(gram_all, lowered)
+    gram_two = doubling_sum(contract_last(basis_one, basis_one), "row")
+    basis_two, upper_two = cholesky_pass(gram_two, basis_one)
     upper_tri = jnp.dot(upper_two, upper_one, precision=HIGHEST_PRECISION)
     basis = math.sqrt(count_all) * basis_two
     return (basis, upper_tri / count_all)

time: 579 us -> 169 us (0.29)
  the two profiles are of different devices: /device:TPU:64 before, /device:TPU:8 now
where the time goes in v1:
time: 169 us; the launch traced here: 168 us
  starting transfers between devices  47.2 us (28%)
  waiting for transfers between devices  42.4 us (25%)
  blocking collectives  25 us (15%)
  other arithmetic  24.9 us (15%)
  matrix products  21.4 us (13%)
  local copies, waits for them, and re-layouts  6.41 us (4%)
    all_to_all x2, starting transfers between devices, exchange(): return lax.all_to_all(blocks, axis, split_axis=0, concat_axis=0, tiled=True)  33.3 us
    all_to_all x2, blocking collectives, exchange(): return lax.all_to_all(blocks, axis, split_axis=0, concat_axis=0, tiled=True)  25 us
    ppermute x5, waiting for transfers between devices, doubling_sum(): lax.ppermute(block, axis, [(i, i ^ step) for i in range(size)])  21.3 us
    all_to_all x2, waiting for transfers between devices, exchange(): return lax.all_to_all(blocks, axis, split_axis=0, concat_axis=0, tiled=True)  21 us
    ppermute x5, starting transfers between devices, doubling_sum(): lax.ppermute(block, axis, [(i, i ^ step) for i in range(size)])  13.3 us
    dot_general x3, matrix products, contract_last(): lax.dot_general(left, right, (((1,), (1,)), ((), ())), precision=HIGHEST_...  9.51 us
    another operation x6, other arithmetic, cholesky_pass(): factor_low = jnp.linalg.cholesky(gram_matrix)  8.73 us
    dot_general x1, matrix products, local(): lax.dot_general(points, embeddings, (((0,), (0,)), ((), ())), precision=H...  8.08 us
  transfers between devices with their start and end apart: 8, of which 7 were waited for; matrix products, arithmetic and copies ran while one was open for 2% of the time, Pallas kernels for 0%

profile of v1, /device:TPU:8, one launch (start us, length us, event | category | flops | bytes accessed | tf_op | source)
XLA Modules:
  0.0 168.3 jit_solution(10131516520279625778)
XLA Ops:
  0.7 0.9 constant_dynamic-slice_fusion
  1.6 0.7 collective-permute-start
  2.2 1.1 reduce_sum.72
  3.4 1.0 reshape.112
  4.4 24.6 %all-to-all-start = ((f32[16,1,4096]{2,1,0:T(1,128)}), f32[16,1,4096]{2,1,0:T(1,128)S(1)}, u32[]{:S(2)}, u32[]{:S(2)}) async-start(f32[16,1,4096]{2,1,0:T(1,128)} %reshape.112), calls=%async_computation | async-start | bytes 524288 | tf_op jit(solution)/shard_map/all_to_all | solution.py:28
  29.1 1.1 multiply_reduce_fusion
  30.2 1.1 broadcast_subtract_fusion
  31.3 9.0 %all-to-all-done = f32[16,1,4096]{2,1,0:T(1,128)S(1)} async-done(((f32[16,1,4096]{2,1,0:T(1,128)}), f32[16,1,4096]{2,1,0:T(1,128)S(1)}, u32[]{:S(2)}, u32[]{:S(2)}) %all-to-all-start) | async-done | bytes 262176 | tf_op jit(solution)/shard_map/all_to_all | solution.py:28
  40.3 0.5 broadcast.105
  40.8 1.3 reduce.9
  42.4 0.3 copy.32
  42.9 8.1 %fusion.47 = f32[1024,2048]{1,0:T(8,128)S(1)} fusion(f32[64,1024]{1,0:T(8,128)S(1)} %reshape.102, f32[64,2048]{1,0:T(8,128)} %param.6), kind=kOutput, calls=%fused_computation.74 | convolution fusion | flops 1610612736 | bytes 9175040 | tf_op jit(solution)/shard_map/dot_general | solution.py:65
  51.0 8.7 %fusion = f32[41,1024]{1,0:T(8,128)S(1)} fusion(f32[1024,2048]{1,0:T(8,128)S(1)} %fusion.47, bf16[1024,2048]{1,0:T(8,128)(2,1)S(1)} %copy-done, f32[2048]{0:T(1024)S(1)} %multiply_reduce_fusion, f32[1024]{0:T(1024)S(1)} %add.64, f32[40,2048]{1,0:T(8,128)S(1)} %broadcast_subtract_fusion), kind=kOutput, calls=%fused_computation | convolution fusion | flops 1042284544 | bytes 13090816 | tf_op jit(solution)/shard_map/dot_general | solution.py:12
  60.2 12.7 %all_to_all.20 = f32[16,1,2688]{2,1,0:T(1,128)S(1)} all-to-all(f32[16,1,2688]{2,1,0:T(1,128)S(1)} %reshape.114), channel_id=1, replica_groups=mesh['row'=32,'col'=16] {'col'}, dimensions={0} | all-to-all | bytes 344064 | tf_op jit(solution)/shard_map/all_to_all | solution.py:28
  72.9 1.0 reduce.10
  74.6 12.3 %all_to_all.21 = f32[16,1,2560]{2,1,0:T(1,128)S(1)} all-to-all(f32[16,1,2560]{2,1,0:T(1,128)S(1)} %reshape.116), channel_id=1, replica_groups=mesh['row'=32,'col'=16] {'col'}, dimensions={0} | all-to-all | bytes 327680 | tf_op jit(solution)/shard_map/all_to_all | solution.py:28
  86.8 1.0 reduce.11
  88.1 0.5 convolution_bitcast_fusion
  88.9 1.2 reshape.118
  90.1 8.6 %all-to-all-start.3 = ((f32[32,1,1640]{2,1,0:T(1,128)}), f32[32,1,1640]{2,1,0:T(1,128)S(1)}, u32[]{:S(2)}, u32[]{:S(2)}) async-start(f32[32,1,1640]{2,1,0:T(1,128)} %reshape.118), calls=%async_computation.3 | async-start | bytes 425984 | tf_op jit(solution)/shard_map/all_to_all | solution.py:28
  98.9 12.0 %all-to-all-done.3 = f32[32,1,1640]{2,1,0:T(1,128)S(1)} async-done(((f32[32,1,1640]{2,1,0:T(1,128)}), f32[32,1,1640]{2,1,0:T(1,128)S(1)}, u32[]{:S(2)}, u32[]{:S(2)}) %all-to-all-start.3) | async-done | bytes 209952 | tf_op jit(solution)/shard_map/all_to_all | solution.py:28
  111.0 1.1 reduce.12
  112.1 0.3 reshape.119
  112.4 0.3 fusion.46
  112.8 0.3 copy.44
  113.1 0.2 fusion.10
  113.4 3.6 %cholesky.44 = f32[40,40]{1,0:T(8,128)S(1)} custom-call(f32[40,40]{1,0:T(8,128)S(1)} %fusion.23), custom_call_target="Cholesky" | custom-call | tf_op jit(solution)/shard_map/jit(cholesky)/cholesky | solution.py:22
  117.1 0.6 compare_reduce_fusion.1
  117.7 0.7 fusion.27
  118.4 3.1 %custom-call.6 = f32[1,40,40]{1,2,0:T(8,128)S(1)} custom-call(f32[1,40,40]{2,1,0:T(8,128)S(1)} %fusion.27), custom_call_target="InvertDiagBlocksLowerTriangular" | custom-call | tf_op jit(solution)/shard_map/triangular_solve/custom-call.0 | solution.py:23
  121.4 0.4 fusion.14
  121.8 0.3 fusion.48
  122.1 1.9 %collective-permute-start.1 = (f32[40,40]{0,1:T(8,128)S(1)}, f32[40,40]{0,1:T(8,128)S(1)}, u32[]{:S(2)}, u32[]{:S(2)}) collective-permute-start(f32[40,40]{0,1:T(8,128)S(1)} %fusion.48), channel_id=1, source_target_pairs={{0,16},{16,0},{32,48},{48,32},{64,80},{80,64},{96,112},{112,96},{1... | collective-permute-start | bytes 19208 | tf_op jit(solution)/shard_map/ppermute | solution.py:39
  124.1 3.7 %collective-permute-done.1 = f32[40,40]{0,1:T(8,128)S(1)} collective-permute-done((f32[40,40]{0,1:T(8,128)S(1)}, f32[40,40]{0,1:T(8,128)S(1)}, u32[]{:S(2)}, u32[]{:S(2)}) %collective-permute-start.1) | collective-permute-done | bytes 6432 | tf_op jit(solution)/shard_map/ppermute | solution.py:39
  127.8 2.8 %collective-permute-start.2 = (f32[40,40]{0,1:T(8,128)S(1)}, f32[40,40]{0,1:T(8,128)S(1)}, u32[]{:S(2)}, u32[]{:S(2)}) collective-permute-start(f32[40,40]{0,1:T(8,128)S(1)} %add.70), channel_id=1, source_target_pairs={{0,32},{16,48},{32,0},{48,16},{64,96},{80,112},{96,64},{112,80},{1... | collective-permute-start | bytes 19208 | tf_op jit(solution)/shard_map/ppermute | solution.py:39
  130.6 3.8 %collective-permute-done.2 = f32[40,40]{0,1:T(8,128)S(1)} collective-permute-done((f32[40,40]{0,1:T(8,128)S(1)}, f32[40,40]{0,1:T(8,128)S(1)}, u32[]{:S(2)}, u32[]{:S(2)}) %collective-permute-start.2) | collective-permute-done | bytes 6432 | tf_op jit(solution)/shard_map/ppermute | solution.py:39
  134.4 2.9 %collective-permute-start.3 = (f32[40,40]{0,1:T(8,128)S(1)}, f32[40,40]{0,1:T(8,128)S(1)}, u32[]{:S(2)}, u32[]{:S(2)}) collective-permute-start(f32[40,40]{0,1:T(8,128)S(1)} %add.71), channel_id=1, source_target_pairs={{0,64},{16,80},{32,96},{48,112},{64,0},{80,16},{96,32},{112,48},{1... | collective-permute-start | bytes 19208 | tf_op jit(solution)/shard_map/ppermute | solution.py:39
  137.3 6.7 %collective-permute-done.3 = f32[40,40]{0,1:T(8,128)S(1)} collective-permute-done((f32[40,40]{0,1:T(8,128)S(1)}, f32[40,40]{0,1:T(8,128)S(1)}, u32[]{:S(2)}, u32[]{:S(2)}) %collective-permute-start.3) | collective-permute-done | bytes 6432 | tf_op jit(solution)/shard_map/ppermute | solution.py:39
  144.0 2.5 %collective-permute-start.4 = (f32[40,40]{0,1:T(8,128)S(1)}, f32[40,40]{0,1:T(8,128)S(1)}, u32[]{:S(2)}, u32[]{:S(2)}) collective-permute-start(f32[40,40]{0,1:T(8,128)S(1)} %add.72), channel_id=1, source_target_pairs={{0,128},{16,144},{32,160},{48,176},{64,192},{80,208},{96,224},{112... | collective-permute-start | bytes 19208 | tf_op jit(solution)/shard_map/ppermute | solution.py:39
  146.5 3.1 %collective-permute-done.4 = f32[40,40]{0,1:T(8,128)S(1)} collective-permute-done((f32[40,40]{0,1:T(8,128)S(1)}, f32[40,40]{0,1:T(8,128)S(1)}, u32[]{:S(2)}, u32[]{:S(2)}) %collective-permute-start.4) | collective-permute-done | bytes 6432 | tf_op jit(solution)/shard_map/ppermute | solution.py:39
  149.6 3.2 %collective-permute-start.5 = (f32[40,40]{0,1:T(8,128)S(1)}, f32[40,40]{0,1:T(8,128)S(1)}, u32[]{:S(2)}, u32[]{:S(2)}) collective-permute-start(f32[40,40]{0,1:T(8,128)S(1)} %add.73), channel_id=1, source_target_pairs={{0,256},{16,272},{32,288},{48,304},{64,320},{80,336},{96,352},{112... | collective-permute-start | bytes 19208 | tf_op jit(solution)/shard_map/ppermute | solution.py:39
  152.8 4.0 %collective-permute-done.5 = f32[40,40]{0,1:T(8,128)S(1)} collective-permute-done((f32[40,40]{0,1:T(8,128)S(1)}, f32[40,40]{0,1:T(8,128)S(1)}, u32[]{:S(2)}, u32[]{:S(2)}) %collective-permute-start.5) | collective-permute-done | bytes 6432 | tf_op jit(solution)/shard_map/ppermute | solution.py:39
  156.9 3.6 %cholesky.55 = f32[40,40]{1,0:T(8,128)S(1)} custom-call(f32[40,40]{1,0:T(8,128)S(1)} %fusion.21), custom_call_target="Cholesky" | custom-call | tf_op jit(solution)/shard_map/jit(cholesky)/cholesky | solution.py:22
  160.6 0.7 compare_reduce_fusion
  161.3 2.2 %convolution_multiply_fusion.1 = f32[40,40]{1,0:T(8,128)} fusion(f32[40,40]{1,0:T(8,128)S(1)} %cholesky.55, f32[40,40]{1,0:T(8,128)S(1)} %cholesky.44, pred[]{:T(512)} %compare_reduce_fusion, pred[]{:T(512)} %compare_reduce_fusion.1), kind=kOutput, calls=%fused_computation.10 | convolution fusion | flops 779200 | bytes 19202 | tf_op jit(solution)/shard_map/dot_general | solution.py:101
  163.5 0.7 select_bitcast_fusion
  164.2 3.1 %custom-call.7 = f32[1,40,40]{1,2,0:T(8,128)S(1)} custom-call(f32[1,40,40]{2,1,0:T(8,128)S(1)} %select_bitcast_fusion), custom_call_target="InvertDiagBlocksLowerTriangular" | custom-call | tf_op jit(solution)/shard_map/triangular_solve/custom-call.0 | solution.py:23
  167.2 1.0 convolution_multiply_fusion
  (44 shorter events, 2.6 us)
Async XLA Ops:
  1.6 1.8 %collective-permute-start = (f32[64,64]{1,0:T(8,128)S(1)}, f32[64,64]{1,0:T(8,128)S(1)}, u32[]{:S(2)}, u32[]{:S(2)}) collective-permute-start(f32[64,64]{1,0:T(8,128)S(1)} %constant_dynamic-slice_fusion), channel_id=1, source_target_pairs={{0,0},{1,32},{2,64},{3,96},{4,128},{5,160},{6,192},{7,224},{8,256}... | collective-permute-start | bytes 49160 | tf_op jit(solution)/shard_map/ppermute | solution.py:60
  4.4 35.8 %all-to-all-start = ((f32[16,1,4096]{2,1,0:T(1,128)}), f32[16,1,4096]{2,1,0:T(1,128)S(1)}, u32[]{:S(2)}, u32[]{:S(2)}) async-start(f32[16,1,4096]{2,1,0:T(1,128)} %reshape.112), calls=%async_computation | async-start | bytes 524288 | tf_op jit(solution)/shard_map/all_to_all | solution.py:28
  42.9 8.1 %copy-start = (bf16[1024,2048]{1,0:T(8,128)(2,1)S(1)}, bf16[1024,2048]{1,0:T(8,128)(2,1)}, u32[]{:S(2)}) copy-start(bf16[1024,2048]{1,0:T(8,128)(2,1)} %param.7) | copy-start | bytes 12582916
  90.1 20.9 %all-to-all-start.3 = ((f32[32,1,1640]{2,1,0:T(1,128)}), f32[32,1,1640]{2,1,0:T(1,128)S(1)}, u32[]{:S(2)}, u32[]{:S(2)}) async-start(f32[32,1,1640]{2,1,0:T(1,128)} %reshape.118), calls=%async_computation.3 | async-start | bytes 425984 | tf_op jit(solution)/shard_map/all_to_all | solution.py:28
  122.1 5.7 %collective-permute-start.1 = (f32[40,40]{0,1:T(8,128)S(1)}, f32[40,40]{0,1:T(8,128)S(1)}, u32[]{:S(2)}, u32[]{:S(2)}) collective-permute-start(f32[40,40]{0,1:T(8,128)S(1)} %fusion.48), channel_id=1, source_target_pairs={{0,16},{16,0},{32,48},{48,32},{64,80},{80,64},{96,112},{112,96},{1... | collective-permute-start | bytes 19208 | tf_op jit(solution)/shard_map/ppermute | solution.py:39
  127.8 6.6 %collective-permute-start.2 = (f32[40,40]{0,1:T(8,128)S(1)}, f32[40,40]{0,1:T(8,128)S(1)}, u32[]{:S(2)}, u32[]{:S(2)}) collective-permute-start(f32[40,40]{0,1:T(8,128)S(1)} %add.70), channel_id=1, source_target_pairs={{0,32},{16,48},{32,0},{48,16},{64,96},{80,112},{96,64},{112,80},{1... | collective-permute-start | bytes 19208 | tf_op jit(solution)/shard_map/ppermute | solution.py:39
  134.4 9.6 %collective-permute-start.3 = (f32[40,40]{0,1:T(8,128)S(1)}, f32[40,40]{0,1:T(8,128)S(1)}, u32[]{:S(2)}, u32[]{:S(2)}) collective-permute-start(f32[40,40]{0,1:T(8,128)S(1)} %add.71), channel_id=1, source_target_pairs={{0,64},{16,80},{32,96},{48,112},{64,0},{80,16},{96,32},{112,48},{1... | collective-permute-start | bytes 19208 | tf_op jit(solution)/shard_map/ppermute | solution.py:39
  144.0 5.7 %collective-permute-start.4 = (f32[40,40]{0,1:T(8,128)S(1)}, f32[40,40]{0,1:T(8,128)S(1)}, u32[]{:S(2)}, u32[]{:S(2)}) collective-permute-start(f32[40,40]{0,1:T(8,128)S(1)} %add.72), channel_id=1, source_target_pairs={{0,128},{16,144},{32,160},{48,176},{64,192},{80,208},{96,224},{112... | collective-permute-start | bytes 19208 | tf_op jit(solution)/shard_map/ppermute | solution.py:39
  149.6 7.2 %collective-permute-start.5 = (f32[40,40]{0,1:T(8,128)S(1)}, f32[40,40]{0,1:T(8,128)S(1)}, u32[]{:S(2)}, u32[]{:S(2)}) collective-permute-start(f32[40,40]{0,1:T(8,128)S(1)} %add.73), channel_id=1, source_target_pairs={{0,256},{16,272},{32,288},{48,304},{64,320},{80,336},{96,352},{112... | collective-permute-start | bytes 19208 | tf_op jit(solution)/shard_map/ppermute | solution.py:39

commit v2 on v0

v2 whole, which is shorter than its diff:
```python
import functools
import math

import jax
import jax.numpy as jnp
from jax import lax
from jax.experimental import pallas as pl
from jax.experimental.pallas import tpu as pltpu
from jax.sharding import PartitionSpec as P

HIGHEST_PRECISION = lax.Precision.HIGHEST
ROW, COL = ("x", "y"), ("z", "core")
LANES = 128
HALF = 64
PACK = 24
ONES = 40
INV = 48
STEP = 256
VMEM = 48 * 1024 * 1024


def dot(left, right, contract, precision=None):
    return lax.dot_general(
        left, right, ((contract[0], contract[1]), ((), ())), precision=precision, preferred_element_type=jnp.float32
    )


def lane_of(shape):
    return lax.broadcasted_iota(jnp.int32, shape, len(shape) - 1)


def row_of(shape):
    return lax.broadcasted_iota(jnp.int32, shape, len(shape) - 2)


def halves_of(values):
    high = values.astype(jnp.bfloat16).astype(jnp.float32)
    return high, values - high


def thirds_of(values):
    first, rest = halves_of(values)
    second, third = halves_of(rest)
    return first, second, third


def one_of(index, choices, other):
    for at, choice in choices.items():
        other = jnp.where(index == at, choice, other)
    return other


def columns_kernel(count, emb_ref, sketch_ref, points_ref, sketch_t_ref, shift_ref, mean_ref):
    emb = emb_ref[...]
    wide = emb.shape[1]
    shift = jnp.sum(emb, axis=1, keepdims=True) * (1.0 / wide)
    shift_ref[...] = jnp.broadcast_to(shift, shift_ref.shape)
    moved = emb - shift
    high, low = halves_of(moved)
    norms = jnp.sum(moved * moved, axis=0, keepdims=True)
    first, second, third = thirds_of(norms)
    at = row_of((16, wide))
    tail = one_of(at, {0: 1.0, 1: 1.0, 2: 1.0, 3: first, 4: second, 5: third}, 0.0)
    points_ref[...] = jnp.concatenate([high, high, low, tail], axis=0).astype(jnp.bfloat16)

    sketch = sketch_ref[...]
    mean = jnp.sum(sketch, axis=1, keepdims=True) * (1.0 / wide)
    high, low = halves_of(sketch - mean)
    ones = jnp.where(row_of((8, wide)) == 0, 1.0, 0.0)
    both = jnp.concatenate([high, ones, low, jnp.zeros((LANES - 88, wide), jnp.float32)], axis=0)
    sketch_t_ref[...] = both.T.astype(jnp.bfloat16)
    across = jnp.concatenate(
        [jnp.broadcast_to(mean, (mean.shape[0], LANES)), jnp.zeros((LANES - mean.shape[0], LANES), jnp.float32)], axis=0
    )
    mean_ref[...] = across.T[:8]


def product_kernel(rows_ref, conf_ref, points_ref, sketch_t_ref, shift_ref, mean_ref, out_ref):
    emb = rows_ref[...].reshape(HALF, STEP)
    moved = emb - shift_ref[:, :1]
    norms = jnp.sum(moved * moved, axis=0, keepdims=True)
    first, second, third = thirds_of(norms)
    high, low = halves_of(-2.0 * moved)
    tail = one_of(row_of((HALF, STEP)), {0: first, 1: second, 2: third, 3: 1.0, 4: 1.0, 5: 1.0}, 0.0)
    left = jnp.concatenate([high, low, high, tail], axis=0).T.astype(jnp.bfloat16)[:, :208]
    total = jnp.zeros((STEP, LANES), jnp.float32)
    wide = conf_ref.shape[1]
    for start in range(0, wide, 256):
        part = slice(start, start + 256)
        distance = dot(left, points_ref[:, part], ((1,), (0,)))
        weighted = conf_ref[:, part].astype(jnp.float32) * distance
        high = weighted.astype(jnp.bfloat16)
        low = (weighted - high.astype(jnp.float32)).astype(jnp.bfloat16)
        right = sketch_t_ref[part, :]
        total = total + dot(high, right, ((1,), (0,))) + dot(low, right, ((1,), (0,)))
    flat = total.T
    flat = flat[:48] + flat[48:96]
    shape = (PACK, LANES)
    lane, row = lane_of(shape), row_of(shape)
    means = jnp.broadcast_to(pltpu.roll(mean_ref[...], HALF, 1)[:1], shape)
    is_mean = (row == ONES + 1 - PACK) & (lane >= HALF)
    for tile in range(STEP // LANES):
        top = flat[:PACK, tile * LANES : (tile + 1) * LANES]
        bottom = flat[PACK:, tile * LANES : (tile + 1) * LANES]
        even = jnp.where(lane < HALF, top, pltpu.roll(bottom, HALF, 1))
        odd = jnp.where(lane < HALF, pltpu.roll(top, HALF, 1), bottom)
        out_ref[2 * tile] = jnp.where(is_mean, means, even)
        out_ref[2 * tile + 1] = jnp.where(is_mean, means, odd)


def piece_kernel(got_ref, out_ref):
    total = got_ref[0]
    for block in range(1, got_ref.shape[0]):
        total = total + got_ref[block]
    sums = pltpu.roll(got_ref[:, ONES - PACK, :], HALF, 1)
    means = pltpu.roll(got_ref[:, ONES + 1 - PACK, :], HALF, 1)
    means = means - jnp.sum(means, axis=0, keepdims=True) * (1.0 / means.shape[0])
    fix = dot(means.T, sums, ((1,), (0,)), HIGHEST_PRECISION)
    shape = (PACK, LANES)
    lane, row = lane_of(shape), row_of(shape)
    total = total + jnp.where(lane < HALF, fix[:PACK], pltpu.roll(fix[PACK : 2 * PACK], HALF, 1))
    below = (lane >= HALF) & (row >= ONES - PACK)
    total = jnp.where(below, jnp.where(row == ONES - PACK, 1.0, 0.0), total)
    out_ref[...] = jnp.broadcast_to(total[None], out_ref.shape)


def unpack(pieces_ref):
    lane = lane_of((PACK, LANES))
    tops, bottoms = [], []
    for at in range(0, pieces_ref.shape[0], 2):
        even, odd = pieces_ref[at], pieces_ref[at + 1]
        tops.append(jnp.where(lane < HALF, even, pltpu.roll(odd, HALF, 1)))
        bottoms.append(jnp.where(lane < HALF, pltpu.roll(even, HALF, 1), odd))
    return jnp.concatenate([jnp.concatenate(tops, axis=1), jnp.concatenate(bottoms, axis=1)], axis=0)


def gram_kernel(pieces_ref, out_ref):
    product = unpack(pieces_ref)
    padded = jnp.concatenate([product, jnp.zeros((LANES - 48, product.shape[1]), jnp.float32)], axis=0)
    gram = dot(product, padded, ((1,), (1,)), HIGHEST_PRECISION)
    lane = lane_of((8, LANES))
    packed = jnp.zeros((8, LANES), jnp.float32)
    for group in range(5):
        rows = gram[8 * group : 8 * group + 8]
        lower = jnp.where(lane < 8 * group + 8, rows, 0.0)
        packed = packed + (pltpu.roll(lower, 4 * group * (group + 1), 1) if group else lower)
        packed = packed + pltpu.roll(jnp.where(lane == ONES, rows, 0.0), 120 + group - ONES, 1)
    out_ref[...] = jnp.broadcast_to(packed[None], out_ref.shape)


def spread_lane(rows, at):
    return jnp.broadcast_to(rows[:, at : at + 1], (8, LANES))


def spread_row(rows, at):
    return jnp.broadcast_to(rows[at : at + 1, :], (8, LANES))


def factor_kernel(count, grams_ref, pieces_ref, basis_ref, upper_ref, bound_ref):
    packed = grams_ref[0]
    for block in range(1, grams_ref.shape[0]):
        packed = packed + grams_ref[block]
    shape = (8, LANES)
    lane, row = lane_of(shape), row_of(shape)
    lowers, sums = [], []
    for group in range(5):
        back = (LANES - 4 * group * (group + 1)) % LANES
        lower = pltpu.roll(packed, back, 1) if back else packed
        lowers.append(jnp.where(lane < 8 * group + 8, lower, 0.0))
        sums.append(jnp.where(lane == ONES, pltpu.roll(packed, LANES + ONES - 120 - group, 1), 0.0))
    square = jnp.concatenate([a + b for a, b in zip(lowers, sums)] + [jnp.zeros((LANES - 40, LANES), jnp.float32)], axis=0)
    flipped = square.T
    ones_row = jnp.where(lane < ONES, spread_row(flipped[ONES : ONES + 8], 0), jnp.where(lane == INV + ONES, 1.0, 0.0))
    groups, trace = [], jnp.zeros((8, 1), jnp.float32)
    for group in range(5):
        upper = jnp.where((lane >= 8 * group + 8) & (lane < ONES), flipped[8 * group : 8 * group + 8], 0.0)
        full = lowers[group] + upper
        diagonal = lane == 8 * group + row
        trace = trace + jnp.sum(jnp.where(diagonal, full, 0.0), axis=1, keepdims=True)
        full = full + jnp.where(lane == INV + 8 * group + row, 1.0, 0.0)
        groups.append(full - (spread_lane(sums[group], ONES) * (1.0 / count)) * ones_row)

    size = jnp.zeros((8, 1), jnp.float32)
    scaled = []
    for block in range(5):
        base = 8 * block
        columns = {i: [spread_lane(groups[i], base + t) for t in range(8)] for i in range(block, 5)}
        rows = [spread_row(groups[block], t) for t in range(8)]
        entry = {(t, s): spread_row(columns[block][s], t) for t in range(8) for s in range(t, 8)}
        result = jnp.zeros(shape, jnp.float32)
        for t in range(8):
            inverse = 1.0 / entry[t, t]
            for s in range(t + 1, 8):
                factor = entry[t, s] * inverse
                for u in range(s, 8):
                    entry[s, u] = entry[s, u] - factor * entry[t, u]
                rows[s] = rows[s] - factor * rows[t]
            for i in range(block + 1, 5):
                factor = columns[i][t] * inverse
                for s in range(t + 1, 8):
                    columns[i][s] = columns[i][s] - factor * entry[t, s]
                groups[i] = groups[i] - factor * rows[t]
            result = jnp.where(row == t, rows[t] * lax.rsqrt(entry[t, t]), result)
        scaled.append(result)
        kept = (lane >= INV) & (lane < INV + ONES)
        size = size + jnp.sum(jnp.where(kept, result * result, 0.0), axis=1, keepdims=True)
        triangle = jnp.where(lane >= base + row, result, 0.0) * (0.5 / count)
        upper_ref[base : base + 8, :] = triangle[:, :40]
    bound = jnp.sum(trace, axis=0, keepdims=True) * jnp.sum(size, axis=0, keepdims=True)
    bound_ref[...] = jnp.broadcast_to(bound, shape)
    solve = jnp.concatenate(scaled, axis=0) * -math.sqrt(count)
    solve = pltpu.roll(solve, LANES - INV, 1)[:, :48]
    basis_ref[...] = dot(solve, unpack(pieces_ref), ((1,), (0,)), HIGHEST_PRECISION)


def call(kernel, outs, flops, *args, **more):
    moved = sum(math.prod(a.shape) * a.dtype.itemsize for a in (*args, *outs))
    return pl.pallas_call(
        kernel,
        out_shape=outs,
        compiler_params=pltpu.CompilerParams(vmem_limit_bytes=VMEM),
        cost_estimate=pl.CostEstimate(flops=flops, bytes_accessed=moved, transcendentals=0),
        **more,
    )(*args)


def array(*shape, dtype=jnp.float32):
    return jax.ShapeDtypeStruct(shape, dtype)


def columns_side(embeddings, sketch):
    wide = embeddings.shape[1]
    outs = (
        array(208, wide, dtype=jnp.bfloat16),
        array(wide, LANES, dtype=jnp.bfloat16),
        array(64, LANES),
        array(8, LANES),
    )
    return call(functools.partial(columns_kernel, wide), outs, 10_000_000, embeddings, sketch)


def product_pieces(rows, confidence, sides):
    row_dev, wide = confidence.shape
    steps = row_dev // STEP
    whole = lambda a: pl.BlockSpec(a.shape, lambda i: (0,) * a.ndim)
    return call(
        product_kernel,
        (array(row_dev // HALF, PACK, LANES),),
        2 * row_dev * wide * (256 + 2 * LANES),
        rows,
        confidence,
        *sides,
        grid=(steps,),
        in_specs=[
            pl.BlockSpec((8, 1, 8, STEP), lambda i: (0, i // 2, 0, i % 2)),
            pl.BlockSpec((STEP, wide), lambda i: (i, 0)),
            *[whole(a) for a in sides],
        ],
        out_specs=(pl.BlockSpec((STEP // HALF, PACK, LANES), lambda i: (i, 0, 0)),),
    )[0]


def piece_sum(got):
    return call(piece_kernel, (array(*got.shape),), 1_000_000, got)[0]


def gram_tile(pieces, copies):
    return call(gram_kernel, (array(copies, 8, LANES),), 40_000_000, pieces)[0]


def factored(grams, pieces, count):
    points = pieces.shape[0] * HALF
    outs = (array(40, points), array(40, 40), array(8, LANES))
    return call(functools.partial(factor_kernel, count), outs, 40_000_000, grams, pieces)


def exchange(blocks, axis):
    return lax.all_to_all(blocks, axis, split_axis=0, concat_axis=0, tiled=True)


def local(embeddings, confidence, sketch):
    n_row, n_col = lax.axis_size(ROW), lax.axis_size(COL)
    row_dev, col_dev = confidence.shape
    count = row_dev * n_row
    halves = col_dev // row_dev
    rindex = lax.axis_index(ROW)

    dims, points = embeddings.shape[0] * 2 // n_col, row_dev // 2
    target = rindex // halves
    mine = lax.dynamic_slice(
        embeddings, (target // 2 * dims, rindex % halves * row_dev + target % 2 * points), (dims, points)
    )
    pairs = [
        (r * n_col + c, (c * halves + r % halves) * n_col + r // halves)
        for r in range(n_row)
        for c in range(n_col)
    ]
    piece = lax.ppermute(mine, ROW + COL, pairs)
    rows = exchange(jnp.broadcast_to(piece[None], (n_col, dims, points)), COL).reshape(-1, 2, dims, points)

    partial_pieces = product_pieces(rows, confidence, columns_side(embeddings, sketch))
    pieces = exchange(piece_sum(exchange(partial_pieces, COL)), COL)
    grams = exchange(gram_tile(pieces, n_row), ROW)
    basis, upper_tri, bound = factored(grams, pieces, count)

    def one_pass():
        return basis, upper_tri

    def two_passes():
        gram = lax.psum(dot(basis, basis, ((1,), (1,)), HIGHEST_PRECISION), ROW) / count
        factor_low = jnp.linalg.cholesky(gram)
        solved = lax.linalg.triangular_solve(factor_low, basis, left_side=True, lower=True)
        return solved, jnp.dot(factor_low.T, upper_tri, precision=HIGHEST_PRECISION)

    return lax.cond(bound[0, 0] < 2.5 * 40 * 40, one_pass, two_passes)


def solution(mesh):
    chips = jax.sharding.Mesh(mesh.devices.reshape(4, 8, 8, 2), ROW + COL)
    placed = (P(None, COL), P(ROW, COL), P(None, COL))
    return jax.shard_map(
        local, mesh=chips, in_specs=placed, out_specs=(P(None, ROW), P()), check_vma=False
    )
```

time: 579 us -> 101 us (0.17)
  the two profiles are of different devices: /device:TPU:64 before, /device:TPU:8 now
where the time goes in v2:
time: 101 us; the launch traced here: 100 us
  blocking collectives  45.2 us (45%)
  starting transfers between devices  26.2 us (26%)
  Pallas kernels  11.1 us (11%)
  waiting for transfers between devices  8.63 us (9%)
  local copies, waits for them, and re-layouts  7.43 us (7%)
  between operations  1.43 us (1%)
    all_to_all x3, blocking collectives, exchange(): return lax.all_to_all(blocks, axis, split_axis=0, concat_axis=0, tiled=True)  45.2 us
    all_to_all x1, starting transfers between devices, exchange(): return lax.all_to_all(blocks, axis, split_axis=0, concat_axis=0, tiled=True)  25.6 us
    pallas_call x5, Pallas kernels, call(): pl.pallas_call(kernel, out_shape=outs, compiler_params=pltpu.CompilerPara...  11.1 us
    all_to_all x1, waiting for transfers between devices, exchange(): return lax.all_to_all(blocks, axis, split_axis=0, concat_axis=0, tiled=True)  8.63 us
    unnamed x10, local copies, waits for them, and re-layouts  5.46 us
  transfers between devices with their start and end apart: 2, of which 1 were waited for; matrix products, arithmetic and copies ran while one was open for 0% of the time, Pallas kernels for 1%

profile of v2, /device:TPU:8, one launch (start us, length us, event | category | flops | bytes accessed | tf_op | source)
XLA Modules:
  0.0 100.0 jit_solution(12182953118305951587)
XLA Ops:
  0.7 0.7 dynamic_slice.3
  1.4 0.7 collective-permute-start
  2.1 0.0 collective-permute-done
  2.1 0.7 broadcast_in_dim.3
  2.8 25.6 %all-to-all-start = ((f32[16,8,512]{2,1,0:T(8,128)}), f32[16,8,512]{2,1,0:T(8,128)S(1)}, u32[]{:S(2)}, u32[]{:S(2)}) async-start(f32[16,8,512]{2,1,0:T(8,128)} %broadcast_in_dim.3), calls=%async_computation | async-start | bytes 524288 | tf_op jit(solution)/shard_map/all_to_all | solution.py:278
  28.4 0.0 copy-start
  28.4 1.0 %copy-done = f32[64,2048]{1,0:T(8,128)S(1)} copy-done((f32[64,2048]{1,0:T(8,128)S(1)}, f32[64,2048]{1,0:T(8,128)}, u32[]{:S(2)}) %copy-start) | copy-done | bytes 524312
  29.4 0.0 copy-start.1
  29.4 1.0 copy-done.1
  30.4 0.5 shard_map.54
  30.9 8.6 %all-to-all-done = f32[16,8,512]{2,1,0:T(8,128)S(1)} async-done(((f32[16,8,512]{2,1,0:T(8,128)}), f32[16,8,512]{2,1,0:T(8,128)S(1)}, u32[]{:S(2)}, u32[]{:S(2)}) %all-to-all-start) | async-done | bytes 262176 | tf_op jit(solution)/shard_map/all_to_all | solution.py:278
  39.6 0.0 copy-start.2
  39.6 2.2 %copy-done.2 = bf16[1024,2048]{1,0:T(8,128)(2,1)S(1)} copy-done((bf16[1024,2048]{1,0:T(8,128)(2,1)S(1)}, bf16[1024,2048]{1,0:T(8,128)(2,1)}, u32[]{:S(2)}) %copy-start.2) | copy-done | bytes 4194328
  41.7 8.1 %shard_map.55 = f32[16,24,128]{2,1,0:T(8,128)S(1)} custom-call(f32[8,2,8,512]{3,2,1,0:T(8,128)S(1)} %bitcast.15, bf16[1024,2048]{1,0:T(8,128)(2,1)S(1)} %copy-done.2, bf16[208,2048]{1,0:T(8,128)(2,1)S(1)} %get-tuple-element.19.points_ref, bf16[2048,128]{1,0:T(8,128)(2,1)S(1)} %get-tuple-element.20.sketch_t_ref, f32[64,128]{1,0:T(8,128)S(1)} %get-tuple-element.21.shift_ref, ...), custom_call_target="tpu_custom_call" | custom-call | flops 2147483648 | bytes 6066176 | tf_op jit(solution)/shard_map/pallas_call | solution.py:218
  49.8 13.2 %all_to_all.20.got_ref = f32[16,24,128]{2,1,0:T(8,128)S(1)} all-to-all(f32[16,24,128]{2,1,0:T(8,128)S(1)} %shard_map.55), channel_id=1, replica_groups=mesh['x'=4,'y'=8,'z'=8,'core'=2] {'z','core'}, dimensions={0} | all-to-all | bytes 393216 | tf_op jit(solution)/shard_map/all_to_all | solution.py:278
  63.0 0.4 shard_map.56
  63.4 13.0 %all_to_all.21.pieces_ref = f32[16,24,128]{2,1,0:T(8,128)S(1)} all-to-all(f32[16,24,128]{2,1,0:T(8,128)S(1)} %shard_map.56), channel_id=1, replica_groups=mesh['x'=4,'y'=8,'z'=8,'core'=2] {'z','core'}, dimensions={0} | all-to-all | bytes 393216 | tf_op jit(solution)/shard_map/all_to_all | solution.py:278
  76.4 0.5 shard_map.57
  76.9 19.1 %all_to_all.22.grams_ref = f32[32,8,128]{2,1,0:T(8,128)S(1)} all-to-all(f32[32,8,128]{2,1,0:T(8,128)S(1)} %shard_map.57), channel_id=1, replica_groups=mesh['x'=4,'y'=8,'z'=8,'core'=2] {'x','y'}, dimensions={0} | all-to-all | bytes 262144 | tf_op jit(solution)/shard_map/all_to_all | solution.py:278
  96.0 1.6 %shard_map.58 = (f32[40,1024]{1,0:T(8,128)S(1)}, f32[40,40]{1,0:T(8,128)S(1)}, f32[8,128]{1,0:T(8,128)S(1)}) custom-call(f32[32,8,128]{2,1,0:T(8,128)S(1)} %all_to_all.22.grams_ref, f32[16,24,128]{2,1,0:T(8,128)S(1)} %all_to_all.21.pieces_ref), custom_call_target="tpu_custom_call" | custom-call | flops 40000000 | bytes 502016 | tf_op jit(solution)/shard_map/pallas_call | solution.py:218
  97.6 0.5 slice.13
  98.8 0.0 copy-start.3
  98.8 0.7 copy-done.3
  99.4 0.0 copy-start.4
  99.4 0.6 copy-done.4
  (1 shorter events, 0.0 us)
Async XLA Ops:
  1.4 0.7 collective-permute-start
  2.8 36.8 %all-to-all-start = ((f32[16,8,512]{2,1,0:T(8,128)}), f32[16,8,512]{2,1,0:T(8,128)S(1)}, u32[]{:S(2)}, u32[]{:S(2)}) async-start(f32[16,8,512]{2,1,0:T(8,128)} %broadcast_in_dim.3), calls=%async_computation | async-start | bytes 524288 | tf_op jit(solution)/shard_map/all_to_all | solution.py:278
  28.4 1.0 %copy-start = (f32[64,2048]{1,0:T(8,128)S(1)}, f32[64,2048]{1,0:T(8,128)}, u32[]{:S(2)}) copy-start(f32[64,2048]{1,0:T(8,128)} %emb_ref.1) | copy-start | bytes 1572868
  29.4 1.0 copy-start.1
  39.6 2.2 %copy-start.2 = (bf16[1024,2048]{1,0:T(8,128)(2,1)S(1)}, bf16[1024,2048]{1,0:T(8,128)(2,1)}, u32[]{:S(2)}) copy-start(bf16[1024,2048]{1,0:T(8,128)(2,1)} %conf_ref.1) | copy-start | bytes 12582916
  98.8 0.7 copy-start.3
  99.4 0.6 copy-start.4

commit v3 on v2

--- a/solution.py
+++ b/solution.py
@@ -1,4 +1,5 @@
 import functools
+import itertools
 import math
 
 import jax
@@ -9,14 +10,16 @@
 from jax.sharding import PartitionSpec as P
 
 HIGHEST_PRECISION = lax.Precision.HIGHEST
-ROW, COL = ("x", "y"), ("z", "core")
+ROW, NEAR = ("x", "y"), ("z_low", "core")
+COL = ("z_high",) + NEAR
 LANES = 128
 HALF = 64
 PACK = 24
 ONES = 40
 INV = 48
-STEP = 256
-VMEM = 48 * 1024 * 1024
+STEP = 512
+CHUNK = 256
+VMEM = 32 * 1024 * 1024
 
 
 def dot(left, right, contract, precision=None):
@@ -50,8 +53,15 @@
     return other
 
 
-def columns_kernel(count, emb_ref, sketch_ref, points_ref, sketch_t_ref, shift_ref, mean_ref):
-    emb = emb_ref[...]
+def columns_kernel(
+    emb_ref, sketch_ref, points_ref, sketch_t_ref, shift_ref, mean_ref, emb_near, sketch_near, emb_sem, sketch_sem
+):
+    emb_copy = pltpu.make_async_copy(emb_ref, emb_near, emb_sem)
+    sketch_copy = pltpu.make_async_copy(sketch_ref, sketch_near, sketch_sem)
+    emb_copy.start()
+    sketch_copy.start()
+    emb_copy.wait()
+    emb = emb_near[...]
     wide = emb.shape[1]
     shift = jnp.sum(emb, axis=1, keepdims=True) * (1.0 / wide)
     shift_ref[...] = jnp.broadcast_to(shift, shift_ref.shape)
@@ -63,7 +73,8 @@
     tail = one_of(at, {0: 1.0, 1: 1.0, 2: 1.0, 3: first, 4: second, 5: third}, 0.0)
     points_ref[...] = jnp.concatenate([high, high, low, tail], axis=0).astype(jnp.bfloat16)
 
-    sketch = sketch_ref[...]
+    sketch_copy.wait()
+    sketch = sketch_near[...]
     mean = jnp.sum(sketch, axis=1, keepdims=True) * (1.0 / wide)
     high, low = halves_of(sketch - mean)
     ones = jnp.where(row_of((8, wide)) == 0, 1.0, 0.0)
@@ -75,37 +86,48 @@
     mean_ref[...] = across.T[:8]
 
 
-def product_kernel(rows_ref, conf_ref, points_ref, sketch_t_ref, shift_ref, mean_ref, out_ref):
-    emb = rows_ref[...].reshape(HALF, STEP)
+def product_kernel(rows_ref, conf_ref, points_ref, sketch_t_ref, shift_ref, mean_ref, out_ref, near_ref, sems):
+    row_dev, wide = conf_ref.shape
+    copies = []
+    for at in range(row_dev // CHUNK):
+        part = pl.ds(at * CHUNK, CHUNK)
+        copies.append(pltpu.make_async_copy(conf_ref.at[part], near_ref.at[part], sems.at[at]))
+        copies[at].start()
+    emb = rows_ref[...].reshape(HALF, row_dev)
     moved = emb - shift_ref[:, :1]
     norms = jnp.sum(moved * moved, axis=0, keepdims=True)
     first, second, third = thirds_of(norms)
     high, low = halves_of(-2.0 * moved)
-    tail = one_of(row_of((HALF, STEP)), {0: first, 1: second, 2: third, 3: 1.0, 4: 1.0, 5: 1.0}, 0.0)
-    left = jnp.concatenate([high, low, high, tail], axis=0).T.astype(jnp.bfloat16)[:, :208]
-    total = jnp.zeros((STEP, LANES), jnp.float32)
-    wide = conf_ref.shape[1]
-    for start in range(0, wide, 256):
-        part = slice(start, start + 256)
-        distance = dot(left, points_ref[:, part], ((1,), (0,)))
-        weighted = conf_ref[:, part].astype(jnp.float32) * distance
-        high = weighted.astype(jnp.bfloat16)
-        low = (weighted - high.astype(jnp.float32)).astype(jnp.bfloat16)
-        right = sketch_t_ref[part, :]
-        total = total + dot(high, right, ((1,), (0,))) + dot(low, right, ((1,), (0,)))
-    flat = total.T
-    flat = flat[:48] + flat[48:96]
+    tail = one_of(row_of((HALF, row_dev)), {0: first, 1: second, 2: third, 3: 1.0, 4: 1.0, 5: 1.0}, 0.0)
+    left = jnp.concatenate([high, low, high, tail], axis=0)
     shape = (PACK, LANES)
     lane, row = lane_of(shape), row_of(shape)
     means = jnp.broadcast_to(pltpu.roll(mean_ref[...], HALF, 1)[:1], shape)
     is_mean = (row == ONES + 1 - PACK) & (lane >= HALF)
-    for tile in range(STEP // LANES):
-        top = flat[:PACK, tile * LANES : (tile + 1) * LANES]
-        bottom = flat[PACK:, tile * LANES : (tile + 1) * LANES]
-        even = jnp.where(lane < HALF, top, pltpu.roll(bottom, HALF, 1))
-        odd = jnp.where(lane < HALF, pltpu.roll(top, HALF, 1), bottom)
-        out_ref[2 * tile] = jnp.where(is_mean, means, even)
-        out_ref[2 * tile + 1] = jnp.where(is_mean, means, odd)
+    for begin in range(0, row_dev, STEP):
+        rows = slice(begin, begin + STEP)
+        for at in range(begin // CHUNK, (begin + STEP) // CHUNK):
+            copies[at].wait()
+        near = left[:, rows].T.astype(jnp.bfloat16)[:, :208]
+        total = jnp.zeros((STEP, LANES), jnp.float32)
+        for start in range(0, wide, 256):
+            part = slice(start, start + 256)
+            distance = dot(near, points_ref[:, part], ((1,), (0,)))
+            weighted = near_ref[rows, part].astype(jnp.float32) * distance
+            high = weighted.astype(jnp.bfloat16)
+            low = (weighted - high.astype(jnp.float32)).astype(jnp.bfloat16)
+            right = sketch_t_ref[part, :]
+            total = total + dot(high, right, ((1,), (0,))) + dot(low, right, ((1,), (0,)))
+        flat = total.T
+        flat = flat[:48] + flat[48:96]
+        for tile in range(STEP // LANES):
+            top = flat[:PACK, tile * LANES : (tile + 1) * LANES]
+            bottom = flat[PACK:, tile * LANES : (tile + 1) * LANES]
+            even = jnp.where(lane < HALF, top, pltpu.roll(bottom, HALF, 1))
+            odd = jnp.where(lane < HALF, pltpu.roll(top, HALF, 1), bottom)
+            at = begin // HALF + 2 * tile
+            out_ref[at] = jnp.where(is_mean, means, even)
+            out_ref[at + 1] = jnp.where(is_mean, means, odd)
 
 
 def piece_kernel(got_ref, out_ref):
@@ -156,7 +178,7 @@
     return jnp.broadcast_to(rows[at : at + 1, :], (8, LANES))
 
 
-def factor_kernel(count, grams_ref, pieces_ref, basis_ref, upper_ref, bound_ref):
+def factor_kernel(count, grams_ref, pieces_ref, basis_ref, upper_ref, small_ref):
     packed = grams_ref[0]
     for block in range(1, grams_ref.shape[0]):
         packed = packed + grams_ref[block]
@@ -206,8 +228,7 @@
         size = size + jnp.sum(jnp.where(kept, result * result, 0.0), axis=1, keepdims=True)
         triangle = jnp.where(lane >= base + row, result, 0.0) * (0.5 / count)
         upper_ref[base : base + 8, :] = triangle[:, :40]
-    bound = jnp.sum(trace, axis=0, keepdims=True) * jnp.sum(size, axis=0, keepdims=True)
-    bound_ref[...] = jnp.broadcast_to(bound, shape)
+    small_ref[0, 0] = (jnp.sum(trace) * jnp.sum(size) < 2.5 * 40 * 40).astype(jnp.int32)
     solve = jnp.concatenate(scaled, axis=0) * -math.sqrt(count)
     solve = pltpu.roll(solve, LANES - INV, 1)[:, :48]
     basis_ref[...] = dot(solve, unpack(pieces_ref), ((1,), (0,)), HIGHEST_PRECISION)
@@ -228,6 +249,10 @@
     return jax.ShapeDtypeStruct(shape, dtype)
 
 
+def far(operand):
+    return pltpu.with_memory_space_constraint(operand, pltpu.HBM)
+
+
 def columns_side(embeddings, sketch):
     wide = embeddings.shape[1]
     outs = (
@@ -236,27 +261,39 @@
         array(64, LANES),
         array(8, LANES),
     )
-    return call(functools.partial(columns_kernel, wide), outs, 10_000_000, embeddings, sketch)
+    return call(
+        columns_kernel,
+        outs,
+        10_000_000,
+        far(embeddings),
+        far(sketch),
+        in_specs=[pl.BlockSpec(memory_space=pltpu.HBM)] * 2,
+        scratch_shapes=[
+            pltpu.VMEM(embeddings.shape, jnp.float32),
+            pltpu.VMEM(sketch.shape, jnp.float32),
+            pltpu.SemaphoreType.DMA,
+            pltpu.SemaphoreType.DMA,
+        ],
+    )
 
 
 def product_pieces(rows, confidence, sides):
     row_dev, wide = confidence.shape
-    steps = row_dev // STEP
-    whole = lambda a: pl.BlockSpec(a.shape, lambda i: (0,) * a.ndim)
+    outs = (array(row_dev // HALF, PACK, LANES),)
+    flops = 2 * row_dev * wide * (256 + 2 * LANES)
+    vmem = pl.BlockSpec(memory_space=pltpu.VMEM)
     return call(
         product_kernel,
-        (array(row_dev // HALF, PACK, LANES),),
-        2 * row_dev * wide * (256 + 2 * LANES),
+        outs,
+        flops,
         rows,
-        confidence,
+        far(confidence),
         *sides,
-        grid=(steps,),
-        in_specs=[
-            pl.BlockSpec((8, 1, 8, STEP), lambda i: (0, i // 2, 0, i % 2)),
-            pl.BlockSpec((STEP, wide), lambda i: (i, 0)),
-            *[whole(a) for a in sides],
+        in_specs=[vmem, pl.BlockSpec(memory_space=pltpu.HBM)] + [vmem] * 4,
+        scratch_shapes=[
+            pltpu.VMEM(confidence.shape, jnp.bfloat16),
+            pltpu.SemaphoreType.DMA((row_dev // CHUNK,)),
         ],
-        out_specs=(pl.BlockSpec((STEP // HALF, PACK, LANES), lambda i: (i, 0, 0)),),
     )[0]
 
 
@@ -270,53 +307,73 @@
 
 def factored(grams, pieces, count):
     points = pieces.shape[0] * HALF
-    outs = (array(40, points), array(40, 40), array(8, LANES))
-    return call(functools.partial(factor_kernel, count), outs, 40_000_000, grams, pieces)
+    outs = (array(40, points), array(40, 40), array(1, 1, dtype=jnp.int32))
+    vmem, smem = (pl.BlockSpec(memory_space=space) for space in (pltpu.VMEM, pltpu.SMEM))
+    return call(
+        functools.partial(factor_kernel, count),
+        outs,
+        40_000_000,
+        grams,
+        pieces,
+        in_specs=[vmem, vmem],
+        out_specs=(vmem, vmem, smem),
+    )
 
 
 def exchange(blocks, axis):
     return lax.all_to_all(blocks, axis, split_axis=0, concat_axis=0, tiled=True)
 
 
+def target_of(x, y, z_high, z_low, core):
+    z = 2 * z_high + z_low
+    to_x, to_y = z // 2, 4 * (z % 2) + 2 * core
+    to_z = (z + 4 + y - to_y + 8) % 8
+    away = (x - to_x + 4) % 4
+    half, to_core = away % 2, away // 2
+    return (to_x, to_y + half, to_z // 2, to_z % 2, to_core), half, to_z % 2 * 2 + to_core
+
+
+def flat_index(at, sizes):
+    index = 0
+    for place, size in zip(at, sizes):
+        index = index * size + place
+    return index
+
+
 def local(embeddings, confidence, sketch):
-    n_row, n_col = lax.axis_size(ROW), lax.axis_size(COL)
-    row_dev, col_dev = confidence.shape
+    n_row, n_near = lax.axis_size(ROW), lax.axis_size(NEAR)
+    row_dev = confidence.shape[0]
     count = row_dev * n_row
-    halves = col_dev // row_dev
-    rindex = lax.axis_index(ROW)
-
-    dims, points = embeddings.shape[0] * 2 // n_col, row_dev // 2
-    target = rindex // halves
-    mine = lax.dynamic_slice(
-        embeddings, (target // 2 * dims, rindex % halves * row_dev + target % 2 * points), (dims, points)
-    )
-    pairs = [
-        (r * n_col + c, (c * halves + r % halves) * n_col + r // halves)
-        for r in range(n_row)
-        for c in range(n_col)
-    ]
-    piece = lax.ppermute(mine, ROW + COL, pairs)
-    rows = exchange(jnp.broadcast_to(piece[None], (n_col, dims, points)), COL).reshape(-1, 2, dims, points)
-
-    partial_pieces = product_pieces(rows, confidence, columns_side(embeddings, sketch))
+
+    dims = embeddings.shape[0] // n_near
+    sizes = tuple(lax.axis_size(axis) for axis in ROW + COL)
+    pairs = []
+    for at in itertools.product(*(range(size) for size in sizes)):
+        pairs.append((flat_index(at, sizes), flat_index(target_of(*at)[0], sizes)))
+    half, part = target_of(*(lax.axis_index(axis) for axis in ROW + COL))[1:]
+    mine = lax.dynamic_slice(embeddings, (part * dims, half * row_dev), (dims, row_dev))
+    mine = lax.ppermute(mine, ROW + COL, pairs)
+    points, sketch_t, shift, mean = columns_side(embeddings, sketch)
+    mine, mean = lax.optimization_barrier((mine, mean))
+    rows = exchange(jnp.broadcast_to(mine[None], (n_near, dims, row_dev)), NEAR)
+
+    partial_pieces = product_pieces(rows, confidence, (points, sketch_t, shift, mean))
     pieces = exchange(piece_sum(exchange(partial_pieces, COL)), COL)
     grams = exchange(gram_tile(pieces, n_row), ROW)
-    basis, upper_tri, bound = factored(grams, pieces, count)
-
-    def one_pass():
-        return basis, upper_tri
-
-    def two_passes():
+    basis, upper_tri, small = factored(grams, pieces, count)
+
+    def second_pass(state):
+        basis, upper_tri, _ = state
         gram = lax.psum(dot(basis, basis, ((1,), (1,)), HIGHEST_PRECISION), ROW) / count
         factor_low = jnp.linalg.cholesky(gram)
         solved = lax.linalg.triangular_solve(factor_low, basis, left_side=True, lower=True)
-        return solved, jnp.dot(factor_low.T, upper_tri, precision=HIGHEST_PRECISION)
-
-    return lax.cond(bound[0, 0] < 2.5 * 40 * 40, one_pass, two_passes)
+        return solved, jnp.dot(factor_low.T, upper_tri, precision=HIGHEST_PRECISION), jnp.int32(1)
+
+    return lax.while_loop(lambda state: state[2] == 0, second_pass, (basis, upper_tri, small[0, 0]))[:2]
 
 
 def solution(mesh):
-    chips = jax.sharding.Mesh(mesh.devices.reshape(4, 8, 8, 2), ROW + COL)
+    chips = jax.sharding.Mesh(mesh.devices.reshape(4, 8, 4, 2, 2), ROW + COL)
     placed = (P(None, COL), P(ROW, COL), P(None, COL))
     return jax.shard_map(
         local, mesh=chips, in_specs=placed, out_specs=(P(None, ROW), P()), check_vma=False

time: 101 us -> 88.8 us (0.88)
  blocking collectives: 45.2 us -> 62.4 us
  starting transfers between devices: 26.2 us -> 10.8 us
  waiting for transfers between devices: 8.63 us -> 0.17 us
  local copies, waits for them, and re-layouts: 7.43 us -> 1.52 us
    all_to_all x1 -> x0, starting transfers between devices: 25.6 us -> none  [exchange(): return lax.all_to_all(blocks, axis, split_axis=0, concat_axis=0, tiled=True)]
    all_to_all x3 -> x4, blocking collectives: 45.2 us -> 62.4 us  [exchange(): return lax.all_to_all(blocks, axis, split_axis=0, concat_axis=0, tiled=True)]
    ppermute x1, starting transfers between devices: 0.65 us -> 10.8 us  [local(): mine = lax.ppermute(mine, ROW + COL, pairs)]
    all_to_all x1 -> x0, waiting for transfers between devices: 8.63 us -> none  [exchange(): return lax.all_to_all(blocks, axis, split_axis=0, concat_axis=0, tiled=True)]
    unnamed x10 -> x4, local copies, waits for them, and re-layouts: 5.46 us -> 0.66 us
    pallas_call x5, Pallas kernels: 11.1 us -> 12.1 us  [call(): pl.pallas_call(kernel, out_shape=outs, compiler_params=pltpu.CompilerPara...]
  transfers between devices with their start and end apart: 2 -> 1, of which waited for: 1 -> 1; matrix products, arithmetic and copies ran while one was open for 0% -> 0% of each run, Pallas kernels for 1% -> 2%
where the time goes in v3:
time: 88.8 us; the launch traced here: 88.5 us
  blocking collectives  62.4 us (70%)
  Pallas kernels  12.1 us (14%)
  starting transfers between devices  10.8 us (12%)
  local copies, waits for them, and re-layouts  1.52 us (2%)
    all_to_all x4, blocking collectives, exchange(): return lax.all_to_all(blocks, axis, split_axis=0, concat_axis=0, tiled=True)  62.4 us
    pallas_call x5, Pallas kernels, call(): pl.pallas_call(kernel, out_shape=outs, compiler_params=pltpu.CompilerPara...  12.1 us
    ppermute x1, starting transfers between devices, local(): mine = lax.ppermute(mine, ROW + COL, pairs)  10.8 us
  transfers between devices with their start and end apart: 1, of which 1 were waited for; matrix products, arithmetic and copies ran while one was open for 0% of the time, Pallas kernels for 2%

profile of v3, /device:TPU:8, one launch (start us, length us, event | category | flops | bytes accessed | tf_op | source)
XLA Modules:
  0.0 88.5 jit_solution(14463986734846921929)
XLA Ops:
  0.7 0.9 dynamic_slice.3
  1.6 10.8 %collective-permute-start = (f32[16,1024]{1,0:T(8,128)S(1)}, f32[16,1024]{1,0:T(8,128)S(1)}, u32[]{:S(2)}, u32[]{:S(2)}) collective-permute-start(f32[16,1024]{1,0:T(8,128)S(1)} %dynamic_slice.3), channel_id=1, source_target_pairs={{0,8},{1,36},{2,66},{3,110},{4,157},{5,185},{6,215},{7,243},{8,257... | collective-permute-start | bytes 196616 | tf_op jit(solution)/shard_map/ppermute | solution.py:355
  12.4 1.7 %shard_map.50 = (bf16[208,2048]{1,0:T(8,128)(2,1)S(1)}, bf16[2048,128]{1,0:T(8,128)(2,1)S(1)}, f32[64,128]{1,0:T(8,128)S(1)}, f32[8,128]{1,0:T(8,128)S(1)}) custom-call(f32[64,2048]{1,0:T(8,128)} %emb_ref.1, f32[40,2048]{1,0:T(8,128)} %sketch_ref.1), custom_call_target="tpu_custom_call" | custom-call | flops 10000000 | bytes 2265088 | tf_op jit(solution)/shard_map/pallas_call | solution.py:239
  14.1 0.2 collective-permute-done
  14.3 8.7 %all_to_all.20.rows_ref = f32[4,16,1024]{2,1,0:T(8,128)S(1)} all-to-all(f32[4,16,1024]{2,1,0:T(8,128)S(1)} %broadcast_in_dim.3), channel_id=1, replica_groups=mesh['x'=4,'y'=8,'z_high'=4,'z_low'=2,'core'=2] {'z_low','core'}, dimensions={0} | all-to-all | bytes 524288 | tf_op jit(solution)/shard_map/all_to_all | solution.py:324
  23.0 7.5 %shard_map.51 = f32[16,24,128]{2,1,0:T(8,128)S(1)} custom-call(f32[4,16,1024]{2,1,0:T(8,128)S(1)} %all_to_all.20.rows_ref, bf16[1024,2048]{1,0:T(8,128)(2,1)} %conf_ref.1, bf16[208,2048]{1,0:T(8,128)(2,1)S(1)} %get-tuple-element.30.points_ref, bf16[2048,128]{1,0:T(8,128)(2,1)S(1)} %get-tuple-element.31.sketch_t_ref, ...), custom_call_target="tpu_custom_call" | custom-call | flops 2147483648 | bytes 6066176 | tf_op jit(solution)/shard_map/pallas_call | solution.py:239
  30.5 19.3 %all_to_all.21.got_ref = f32[16,24,128]{2,1,0:T(8,128)S(1)} all-to-all(f32[16,24,128]{2,1,0:T(8,128)S(1)} %shard_map.51), channel_id=1, replica_groups=mesh['x'=4,'y'=8,'z_high'=4,'z_low'=2,'core'=2] {'z_high','z_low','core'}, dimensions={0} | all-to-all | bytes 393216 | tf_op jit(solution)/shard_map/all_to_all | solution.py:324
  49.8 0.4 shard_map.52
  50.2 13.0 %all_to_all.22.pieces_ref = f32[16,24,128]{2,1,0:T(8,128)S(1)} all-to-all(f32[16,24,128]{2,1,0:T(8,128)S(1)} %shard_map.52), channel_id=1, replica_groups=mesh['x'=4,'y'=8,'z_high'=4,'z_low'=2,'core'=2] {'z_high','z_low','core'}, dimensions={0} | all-to-all | bytes 393216 | tf_op jit(solution)/shard_map/all_to_all | solution.py:324
  63.2 0.5 shard_map.53
  63.7 21.4 %all_to_all.23.grams_ref = f32[32,8,128]{2,1,0:T(8,128)S(1)} all-to-all(f32[32,8,128]{2,1,0:T(8,128)S(1)} %shard_map.53), channel_id=1, replica_groups=mesh['x'=4,'y'=8,'z_high'=4,'z_low'=2,'core'=2] {'x','y'}, dimensions={0} | all-to-all | bytes 262144 | tf_op jit(solution)/shard_map/all_to_all | solution.py:324
  85.1 2.1 %shard_map.54 = (f32[40,1024]{1,0:T(8,128)S(1)}, f32[40,40]{1,0:T(8,128)S(1)}, s32[1,1]{1,0:T(1,128)}) custom-call(f32[32,8,128]{2,1,0:T(8,128)S(1)} %all_to_all.23.grams_ref, f32[16,24,128]{2,1,0:T(8,128)S(1)} %all_to_all.22.pieces_ref), custom_call_target="tpu_custom_call" | custom-call | flops 40000000 | bytes 497924 | tf_op jit(solution)/shard_map/pallas_call | solution.py:239
  87.1 0.7 while.11
  87.8 0.0 copy-start
  87.8 0.0 copy-start.1
  87.8 0.6 copy-done
  88.5 0.0 copy-done.1
  (1 shorter events, 0.0 us)
Async XLA Ops:
  1.6 12.7 %collective-permute-start = (f32[16,1024]{1,0:T(8,128)S(1)}, f32[16,1024]{1,0:T(8,128)S(1)}, u32[]{:S(2)}, u32[]{:S(2)}) collective-permute-start(f32[16,1024]{1,0:T(8,128)S(1)} %dynamic_slice.3), channel_id=1, source_target_pairs={{0,8},{1,36},{2,66},{3,110},{4,157},{5,185},{6,215},{7,243},{8,257... | collective-permute-start | bytes 196616 | tf_op jit(solution)/shard_map/ppermute | solution.py:355
  87.8 0.7 copy-start
  87.8 0.7 copy-start.1

commit v4 on v3

--- a/solution.py
+++ b/solution.py
@@ -17,8 +17,7 @@
 PACK = 24
 ONES = 40
 INV = 48
-STEP = 512
-CHUNK = 256
+STEP = 1024
 VMEM = 32 * 1024 * 1024
 
 
@@ -54,12 +53,14 @@
 
 
 def columns_kernel(
-    emb_ref, sketch_ref, points_ref, sketch_t_ref, shift_ref, mean_ref, emb_near, sketch_near, emb_sem, sketch_sem
+    emb_ref, sketch_ref, conf_ref, points_ref, sketch_t_ref, shift_ref, mean_ref, conf_near, emb_near, sketch_near, sems
 ):
-    emb_copy = pltpu.make_async_copy(emb_ref, emb_near, emb_sem)
-    sketch_copy = pltpu.make_async_copy(sketch_ref, sketch_near, sketch_sem)
+    emb_copy = pltpu.make_async_copy(emb_ref, emb_near, sems.at[0])
+    sketch_copy = pltpu.make_async_copy(sketch_ref, sketch_near, sems.at[1])
+    conf_copy = pltpu.make_async_copy(conf_ref, conf_near, sems.at[2])
     emb_copy.start()
     sketch_copy.start()
+    conf_copy.start()
     emb_copy.wait()
     emb = emb_near[...]
     wide = emb.shape[1]
@@ -84,15 +85,11 @@
         [jnp.broadcast_to(mean, (mean.shape[0], LANES)), jnp.zeros((LANES - mean.shape[0], LANES), jnp.float32)], axis=0
     )
     mean_ref[...] = across.T[:8]
-
-
-def product_kernel(rows_ref, conf_ref, points_ref, sketch_t_ref, shift_ref, mean_ref, out_ref, near_ref, sems):
+    conf_copy.wait()
+
+
+def product_kernel(rows_ref, conf_ref, points_ref, sketch_t_ref, shift_ref, mean_ref, out_ref):
     row_dev, wide = conf_ref.shape
-    copies = []
-    for at in range(row_dev // CHUNK):
-        part = pl.ds(at * CHUNK, CHUNK)
-        copies.append(pltpu.make_async_copy(conf_ref.at[part], near_ref.at[part], sems.at[at]))
-        copies[at].start()
     emb = rows_ref[...].reshape(HALF, row_dev)
     moved = emb - shift_ref[:, :1]
     norms = jnp.sum(moved * moved, axis=0, keepdims=True)
@@ -106,14 +103,12 @@
     is_mean = (row == ONES + 1 - PACK) & (lane >= HALF)
     for begin in range(0, row_dev, STEP):
         rows = slice(begin, begin + STEP)
-        for at in range(begin // CHUNK, (begin + STEP) // CHUNK):
-            copies[at].wait()
         near = left[:, rows].T.astype(jnp.bfloat16)[:, :208]
         total = jnp.zeros((STEP, LANES), jnp.float32)
         for start in range(0, wide, 256):
             part = slice(start, start + 256)
             distance = dot(near, points_ref[:, part], ((1,), (0,)))
-            weighted = near_ref[rows, part].astype(jnp.float32) * distance
+            weighted = conf_ref[rows, part].astype(jnp.float32) * distance
             high = weighted.astype(jnp.bfloat16)
             low = (weighted - high.astype(jnp.float32)).astype(jnp.bfloat16)
             right = sketch_t_ref[part, :]
@@ -178,7 +173,7 @@
     return jnp.broadcast_to(rows[at : at + 1, :], (8, LANES))
 
 
-def factor_kernel(count, grams_ref, pieces_ref, basis_ref, upper_ref, small_ref):
+def factor_kernel(count, grams_ref, pieces_ref, basis_ref, upper_ref, small_ref, basis_near, upper_near, sems):
     packed = grams_ref[0]
     for block in range(1, grams_ref.shape[0]):
         packed = packed + grams_ref[block]
@@ -227,11 +222,17 @@
         kept = (lane >= INV) & (lane < INV + ONES)
         size = size + jnp.sum(jnp.where(kept, result * result, 0.0), axis=1, keepdims=True)
         triangle = jnp.where(lane >= base + row, result, 0.0) * (0.5 / count)
-        upper_ref[base : base + 8, :] = triangle[:, :40]
-    small_ref[0, 0] = (jnp.sum(trace) * jnp.sum(size) < 2.5 * 40 * 40).astype(jnp.int32)
+        upper_near[base : base + 8, :] = triangle[:, :40]
+    upper_copy = pltpu.make_async_copy(upper_near, upper_ref, sems.at[0])
+    upper_copy.start()
     solve = jnp.concatenate(scaled, axis=0) * -math.sqrt(count)
     solve = pltpu.roll(solve, LANES - INV, 1)[:, :48]
-    basis_ref[...] = dot(solve, unpack(pieces_ref), ((1,), (0,)), HIGHEST_PRECISION)
+    basis_near[...] = dot(solve, unpack(pieces_ref), ((1,), (0,)), HIGHEST_PRECISION)
+    basis_copy = pltpu.make_async_copy(basis_near, basis_ref, sems.at[1])
+    basis_copy.start()
+    small_ref[0, 0] = (jnp.sum(trace) * jnp.sum(size) < 2.5 * 40 * 40).astype(jnp.int32)
+    upper_copy.wait()
+    basis_copy.wait()
 
 
 def call(kernel, outs, flops, *args, **more):
@@ -253,13 +254,14 @@
     return pltpu.with_memory_space_constraint(operand, pltpu.HBM)
 
 
-def columns_side(embeddings, sketch):
+def columns_side(embeddings, sketch, confidence):
     wide = embeddings.shape[1]
     outs = (
         array(208, wide, dtype=jnp.bfloat16),
         array(wide, LANES, dtype=jnp.bfloat16),
         array(64, LANES),
         array(8, LANES),
+        pltpu.VMEM(confidence.shape, jnp.bfloat16),
     )
     return call(
         columns_kernel,
@@ -267,34 +269,24 @@
         10_000_000,
         far(embeddings),
         far(sketch),
-        in_specs=[pl.BlockSpec(memory_space=pltpu.HBM)] * 2,
+        far(confidence),
+        in_specs=[pl.BlockSpec(memory_space=pltpu.HBM)] * 3,
+        out_specs=(pl.BlockSpec(memory_space=pltpu.VMEM),) * 5,
         scratch_shapes=[
             pltpu.VMEM(embeddings.shape, jnp.float32),
             pltpu.VMEM(sketch.shape, jnp.float32),
-            pltpu.SemaphoreType.DMA,
-            pltpu.SemaphoreType.DMA,
+            pltpu.SemaphoreType.DMA((3,)),
         ],
     )
 
 
-def product_pieces(rows, confidence, sides):
+def product_pieces(rows, sides):
+    points, sketch_t, shift, mean, confidence = sides
     row_dev, wide = confidence.shape
     outs = (array(row_dev // HALF, PACK, LANES),)
     flops = 2 * row_dev * wide * (256 + 2 * LANES)
-    vmem = pl.BlockSpec(memory_space=pltpu.VMEM)
-    return call(
-        product_kernel,
-        outs,
-        flops,
-        rows,
-        far(confidence),
-        *sides,
-        in_specs=[vmem, pl.BlockSpec(memory_space=pltpu.HBM)] + [vmem] * 4,
-        scratch_shapes=[
-            pltpu.VMEM(confidence.shape, jnp.bfloat16),
-            pltpu.SemaphoreType.DMA((row_dev // CHUNK,)),
-        ],
-    )[0]
+    confidence = pltpu.with_memory_space_constraint(confidence, pltpu.VMEM)
+    return call(product_kernel, outs, flops, rows, confidence, points, sketch_t, shift, mean)[0]
 
 
 def piece_sum(got):
@@ -307,8 +299,8 @@
 
 def factored(grams, pieces, count):
     points = pieces.shape[0] * HALF
-    outs = (array(40, points), array(40, 40), array(1, 1, dtype=jnp.int32))
-    vmem, smem = (pl.BlockSpec(memory_space=space) for space in (pltpu.VMEM, pltpu.SMEM))
+    outs = (pltpu.HBM((40, points), jnp.float32), pltpu.HBM((40, 40), jnp.float32), array(1, 1, dtype=jnp.int32))
+    vmem, smem, hbm = (pl.BlockSpec(memory_space=space) for space in (pltpu.VMEM, pltpu.SMEM, pltpu.HBM))
     return call(
         functools.partial(factor_kernel, count),
         outs,
@@ -316,7 +308,12 @@
         grams,
         pieces,
         in_specs=[vmem, vmem],
-        out_specs=(vmem, vmem, smem),
+        out_specs=(hbm, hbm, smem),
+        scratch_shapes=[
+            pltpu.VMEM((40, points), jnp.float32),
+            pltpu.VMEM((40, 40), jnp.float32),
+            pltpu.SemaphoreType.DMA((2,)),
+        ],
     )
 
 
@@ -353,11 +350,11 @@
     half, part = target_of(*(lax.axis_index(axis) for axis in ROW + COL))[1:]
     mine = lax.dynamic_slice(embeddings, (part * dims, half * row_dev), (dims, row_dev))
     mine = lax.ppermute(mine, ROW + COL, pairs)
-    points, sketch_t, shift, mean = columns_side(embeddings, sketch)
+    points, sketch_t, shift, mean, near = columns_side(embeddings, sketch, confidence)
     mine, mean = lax.optimization_barrier((mine, mean))
     rows = exchange(jnp.broadcast_to(mine[None], (n_near, dims, row_dev)), NEAR)
 
-    partial_pieces = product_pieces(rows, confidence, (points, sketch_t, shift, mean))
+    partial_pieces = product_pieces(rows, (points, sketch_t, shift, mean, near))
     pieces = exchange(piece_sum(exchange(partial_pieces, COL)), COL)
     grams = exchange(gram_tile(pieces, n_row), ROW)
     basis, upper_tri, small = factored(grams, pieces, count)

time: 88.8 us -> 86.9 us (0.979)
  transfers between devices with their start and end apart: 1 -> 1, of which waited for: 1 -> 0; matrix products, arithmetic and copies ran while one was open for 0% -> 0% of each run, Pallas kernels for 2% -> 3%
where the time goes in v4:
time: 86.9 us; the launch traced here: 86.6 us
  blocking collectives  61.7 us (71%)
  Pallas kernels  11.8 us (14%)
  starting transfers between devices  10.8 us (12%)
  local copies, waits for them, and re-layouts  0.87 us (1%)
    all_to_all x4, blocking collectives, exchange(): return lax.all_to_all(blocks, axis, split_axis=0, concat_axis=0, tiled=True)  61.7 us
    pallas_call x5, Pallas kernels, call(): pl.pallas_call(kernel, out_shape=outs, compiler_params=pltpu.CompilerPara...  11.8 us
    ppermute x1, starting transfers between devices, local(): mine = lax.ppermute(mine, ROW + COL, pairs)  10.8 us
  transfers between devices with their start and end apart: 1, of which 0 were waited for; matrix products, arithmetic and copies ran while one was open for 0% of the time, Pallas kernels for 3%

profile of v4, /device:TPU:8, one launch (start us, length us, event | category | flops | bytes accessed | tf_op | source)
XLA Modules:
  0.0 86.6 jit_solution(6136730087971989482)
XLA Ops:
  0.7 0.9 dynamic_slice.3
  1.6 10.8 %collective-permute-start = (f32[16,1024]{1,0:T(8,128)S(1)}, f32[16,1024]{1,0:T(8,128)S(1)}, u32[]{:S(2)}, u32[]{:S(2)}) collective-permute-start(f32[16,1024]{1,0:T(8,128)S(1)} %dynamic_slice.3), channel_id=1, source_target_pairs={{0,8},{1,36},{2,66},{3,110},{4,157},{5,185},{6,215},{7,243},{8,257... | collective-permute-start | bytes 196616 | tf_op jit(solution)/shard_map/ppermute | solution.py:352
  12.4 2.5 %shard_map.50 = (bf16[208,2048]{1,0:T(8,128)(2,1)S(1)}, bf16[2048,128]{1,0:T(8,128)(2,1)S(1)}, f32[64,128]{1,0:T(8,128)S(1)}, f32[8,128]{1,0:T(8,128)S(1)}, bf16[1024,2048]{1,0:T(8,128)(2,1)S(1)}) custom-call(f32[64,2048]{1,0:T(8,128)} %emb_ref.1, f32[40,2048]{1,0:T(8,128)} %sketch_ref.1, bf16[1024,2048]{1,0:T(8,128)(2,1)} %conf_ref.1), custom_call_target="tpu_custom_call" | custom-call | flops 10000000 | bytes 10653696 | tf_op jit(solution)/shard_map/pallas_call | solution.py:240
  14.9 0.0 collective-permute-done
  14.9 8.4 %all_to_all.20.rows_ref = f32[4,16,1024]{2,1,0:T(8,128)S(1)} all-to-all(f32[4,16,1024]{2,1,0:T(8,128)S(1)} %broadcast_in_dim.3), channel_id=1, replica_groups=mesh['x'=4,'y'=8,'z_high'=4,'z_low'=2,'core'=2] {'z_low','core'}, dimensions={0} | all-to-all | bytes 524288 | tf_op jit(solution)/shard_map/all_to_all | solution.py:321
  23.4 5.6 %shard_map.51 = f32[16,24,128]{2,1,0:T(8,128)S(1)} custom-call(f32[4,16,1024]{2,1,0:T(8,128)S(1)} %all_to_all.20.rows_ref, bf16[1024,2048]{1,0:T(8,128)(2,1)S(1)} %get-tuple-element.31.conf_ref, bf16[208,2048]{1,0:T(8,128)(2,1)S(1)} %get-tuple-element.32.points_ref, bf16[2048,128]{1,0:T(8,128)(2,1)S(1)} %get-tuple-element.33.sketch_t_ref, ...), custom_call_target="tpu_custom_call" | custom-call | flops 2147483648 | bytes 6066176 | tf_op jit(solution)/shard_map/pallas_call | solution.py:240
  29.0 19.0 %all_to_all.21.got_ref = f32[16,24,128]{2,1,0:T(8,128)S(1)} all-to-all(f32[16,24,128]{2,1,0:T(8,128)S(1)} %shard_map.51), channel_id=1, replica_groups=mesh['x'=4,'y'=8,'z_high'=4,'z_low'=2,'core'=2] {'z_high','z_low','core'}, dimensions={0} | all-to-all | bytes 393216 | tf_op jit(solution)/shard_map/all_to_all | solution.py:321
  48.0 0.4 shard_map.52
  48.4 13.0 %all_to_all.22.pieces_ref = f32[16,24,128]{2,1,0:T(8,128)S(1)} all-to-all(f32[16,24,128]{2,1,0:T(8,128)S(1)} %shard_map.52), channel_id=1, replica_groups=mesh['x'=4,'y'=8,'z_high'=4,'z_low'=2,'core'=2] {'z_high','z_low','core'}, dimensions={0} | all-to-all | bytes 393216 | tf_op jit(solution)/shard_map/all_to_all | solution.py:321
  61.4 0.5 shard_map.53
  61.9 21.3 %all_to_all.23.grams_ref = f32[32,8,128]{2,1,0:T(8,128)S(1)} all-to-all(f32[32,8,128]{2,1,0:T(8,128)S(1)} %shard_map.53), channel_id=1, replica_groups=mesh['x'=4,'y'=8,'z_high'=4,'z_low'=2,'core'=2] {'x','y'}, dimensions={0} | all-to-all | bytes 262144 | tf_op jit(solution)/shard_map/all_to_all | solution.py:321
  83.2 2.8 %shard_map.54 = (f32[40,1024]{1,0:T(8,128)}, f32[40,40]{1,0:T(8,128)}, s32[1,1]{1,0:T(1,128)}) custom-call(f32[32,8,128]{2,1,0:T(8,128)S(1)} %all_to_all.23.grams_ref, f32[16,24,128]{2,1,0:T(8,128)S(1)} %all_to_all.22.pieces_ref), custom_call_target="tpu_custom_call" | custom-call | flops 40000000 | bytes 497924 | tf_op jit(solution)/shard_map/pallas_call | solution.py:240
  86.0 0.6 while.11
  (1 shorter events, 0.0 us)
Async XLA Ops:
  1.6 13.3 %collective-permute-start = (f32[16,1024]{1,0:T(8,128)S(1)}, f32[16,1024]{1,0:T(8,128)S(1)}, u32[]{:S(2)}, u32[]{:S(2)}) collective-permute-start(f32[16,1024]{1,0:T(8,128)S(1)} %dynamic_slice.3), channel_id=1, source_target_pairs={{0,8},{1,36},{2,66},{3,110},{4,157},{5,185},{6,215},{7,243},{8,257... | collective-permute-start | bytes 196616 | tf_op jit(solution)/shard_map/ppermute | solution.py:352

commit v5 on v4

--- a/solution.py
+++ b/solution.py
@@ -17,7 +17,7 @@
 PACK = 24
 ONES = 40
 INV = 48
-STEP = 1024
+STEP = 256
 VMEM = 32 * 1024 * 1024
 
 
@@ -227,12 +227,18 @@
     upper_copy.start()
     solve = jnp.concatenate(scaled, axis=0) * -math.sqrt(count)
     solve = pltpu.roll(solve, LANES - INV, 1)[:, :48]
-    basis_near[...] = dot(solve, unpack(pieces_ref), ((1,), (0,)), HIGHEST_PRECISION)
-    basis_copy = pltpu.make_async_copy(basis_near, basis_ref, sems.at[1])
-    basis_copy.start()
+    product = unpack(pieces_ref)
+    basis_copies = []
+    for half in range(2):
+        part = pl.ds(half * (product.shape[1] // 2), product.shape[1] // 2)
+        columns = product[:, half * part.size : (half + 1) * part.size]
+        basis_near[:, part] = dot(solve, columns, ((1,), (0,)), HIGHEST_PRECISION)
+        basis_copies.append(pltpu.make_async_copy(basis_near.at[:, part], basis_ref.at[:, part], sems.at[1 + half]))
+        basis_copies[half].start()
     small_ref[0, 0] = (jnp.sum(trace) * jnp.sum(size) < 2.5 * 40 * 40).astype(jnp.int32)
     upper_copy.wait()
-    basis_copy.wait()
+    for copy in basis_copies:
+        copy.wait()
 
 
 def call(kernel, outs, flops, *args, **more):
@@ -312,7 +318,7 @@
         scratch_shapes=[
             pltpu.VMEM((40, points), jnp.float32),
             pltpu.VMEM((40, 40), jnp.float32),
-            pltpu.SemaphoreType.DMA((2,)),
+            pltpu.SemaphoreType.DMA((3,)),
         ],
     )
 

time: 86.9 us -> 88.4 us (1.017)
  Pallas kernels: 11.8 us -> 13.3 us
    pallas_call x5, Pallas kernels: 11.8 us -> 13.3 us  [call(): pl.pallas_call(kernel, out_shape=outs, compiler_params=pltpu.CompilerPara...]
where the time goes in v5:
time: 88.4 us; the launch traced here: 88.1 us
  blocking collectives  61.7 us (70%)
  Pallas kernels  13.3 us (15%)
  starting transfers between devices  10.8 us (12%)
    all_to_all x4, blocking collectives, exchange(): return lax.all_to_all(blocks, axis, split_axis=0, concat_axis=0, tiled=True)  61.7 us
    pallas_call x5, Pallas kernels, call(): pl.pallas_call(kernel, out_shape=outs, compiler_params=pltpu.CompilerPara...  13.3 us
    ppermute x1, starting transfers between devices, local(): mine = lax.ppermute(mine, ROW + COL, pairs)  10.8 us
  transfers between devices with their start and end apart: 1, of which 0 were waited for; matrix products, arithmetic and copies ran while one was open for 0% of the time, Pallas kernels for 3%

profile of v5, /device:TPU:8, one launch (start us, length us, event | category | flops | bytes accessed | tf_op | source)
XLA Modules:
  0.0 88.1 jit_solution(11804298189723205448)
XLA Ops:
  0.7 0.9 dynamic_slice.3
  1.6 10.8 %collective-permute-start = (f32[16,1024]{1,0:T(8,128)S(1)}, f32[16,1024]{1,0:T(8,128)S(1)}, u32[]{:S(2)}, u32[]{:S(2)}) collective-permute-start(f32[16,1024]{1,0:T(8,128)S(1)} %dynamic_slice.3), channel_id=1, source_target_pairs={{0,8},{1,36},{2,66},{3,110},{4,157},{5,185},{6,215},{7,243},{8,257... | collective-permute-start | bytes 196616 | tf_op jit(solution)/shard_map/ppermute | solution.py:358
  12.4 2.5 %shard_map.50 = (bf16[208,2048]{1,0:T(8,128)(2,1)S(1)}, bf16[2048,128]{1,0:T(8,128)(2,1)S(1)}, f32[64,128]{1,0:T(8,128)S(1)}, f32[8,128]{1,0:T(8,128)S(1)}, bf16[1024,2048]{1,0:T(8,128)(2,1)S(1)}) custom-call(f32[64,2048]{1,0:T(8,128)} %emb_ref.1, f32[40,2048]{1,0:T(8,128)} %sketch_ref.1, bf16[1024,2048]{1,0:T(8,128)(2,1)} %conf_ref.1), custom_call_target="tpu_custom_call" | custom-call | flops 10000000 | bytes 10653696 | tf_op jit(solution)/shard_map/pallas_call | solution.py:246
  14.9 0.0 collective-permute-done
  14.9 8.4 %all_to_all.20.rows_ref = f32[4,16,1024]{2,1,0:T(8,128)S(1)} all-to-all(f32[4,16,1024]{2,1,0:T(8,128)S(1)} %broadcast_in_dim.3), channel_id=1, replica_groups=mesh['x'=4,'y'=8,'z_high'=4,'z_low'=2,'core'=2] {'z_low','core'}, dimensions={0} | all-to-all | bytes 524288 | tf_op jit(solution)/shard_map/all_to_all | solution.py:327
  23.4 7.2 %shard_map.51 = f32[16,24,128]{2,1,0:T(8,128)S(1)} custom-call(f32[4,16,1024]{2,1,0:T(8,128)S(1)} %all_to_all.20.rows_ref, bf16[1024,2048]{1,0:T(8,128)(2,1)S(1)} %get-tuple-element.31.conf_ref, bf16[208,2048]{1,0:T(8,128)(2,1)S(1)} %get-tuple-element.32.points_ref, bf16[2048,128]{1,0:T(8,128)(2,1)S(1)} %get-tuple-element.33.sketch_t_ref, ...), custom_call_target="tpu_custom_call" | custom-call | flops 2147483648 | bytes 6066176 | tf_op jit(solution)/shard_map/pallas_call | solution.py:246
  30.5 19.0 %all_to_all.21.got_ref = f32[16,24,128]{2,1,0:T(8,128)S(1)} all-to-all(f32[16,24,128]{2,1,0:T(8,128)S(1)} %shard_map.51), channel_id=1, replica_groups=mesh['x'=4,'y'=8,'z_high'=4,'z_low'=2,'core'=2] {'z_high','z_low','core'}, dimensions={0} | all-to-all | bytes 393216 | tf_op jit(solution)/shard_map/all_to_all | solution.py:327
  49.5 0.4 shard_map.52
  50.0 13.0 %all_to_all.22.pieces_ref = f32[16,24,128]{2,1,0:T(8,128)S(1)} all-to-all(f32[16,24,128]{2,1,0:T(8,128)S(1)} %shard_map.52), channel_id=1, replica_groups=mesh['x'=4,'y'=8,'z_high'=4,'z_low'=2,'core'=2] {'z_high','z_low','core'}, dimensions={0} | all-to-all | bytes 393216 | tf_op jit(solution)/shard_map/all_to_all | solution.py:327
  63.0 0.5 shard_map.53
  63.4 21.3 %all_to_all.23.grams_ref = f32[32,8,128]{2,1,0:T(8,128)S(1)} all-to-all(f32[32,8,128]{2,1,0:T(8,128)S(1)} %shard_map.53), channel_id=1, replica_groups=mesh['x'=4,'y'=8,'z_high'=4,'z_low'=2,'core'=2] {'x','y'}, dimensions={0} | all-to-all | bytes 262144 | tf_op jit(solution)/shard_map/all_to_all | solution.py:327
  84.7 2.8 %shard_map.54 = (f32[40,1024]{1,0:T(8,128)}, f32[40,40]{1,0:T(8,128)}, s32[1,1]{1,0:T(1,128)}) custom-call(f32[32,8,128]{2,1,0:T(8,128)S(1)} %all_to_all.23.grams_ref, f32[16,24,128]{2,1,0:T(8,128)S(1)} %all_to_all.22.pieces_ref), custom_call_target="tpu_custom_call" | custom-call | flops 40000000 | bytes 497924 | tf_op jit(solution)/shard_map/pallas_call | solution.py:246
  87.5 0.6 while.11
  (1 shorter events, 0.0 us)
Async XLA Ops:
  1.6 13.3 %collective-permute-start = (f32[16,1024]{1,0:T(8,128)S(1)}, f32[16,1024]{1,0:T(8,128)S(1)}, u32[]{:S(2)}, u32[]{:S(2)}) collective-permute-start(f32[16,1024]{1,0:T(8,128)S(1)} %dynamic_slice.3), channel_id=1, source_target_pairs={{0,8},{1,36},{2,66},{3,110},{4,157},{5,185},{6,215},{7,243},{8,257... | collective-permute-start | bytes 196616 | tf_op jit(solution)/shard_map/ppermute | solution.py:358

commit v6 on v5

--- a/solution.py
+++ b/solution.py
@@ -17,7 +17,7 @@
 PACK = 24
 ONES = 40
 INV = 48
-STEP = 256
+STEP = 512
 VMEM = 32 * 1024 * 1024
 
 
@@ -111,8 +111,8 @@
             weighted = conf_ref[rows, part].astype(jnp.float32) * distance
             high = weighted.astype(jnp.bfloat16)
             low = (weighted - high.astype(jnp.float32)).astype(jnp.bfloat16)
-            right = sketch_t_ref[part, :]
-            total = total + dot(high, right, ((1,), (0,))) + dot(low, right, ((1,), (0,)))
+            both = dot(jnp.concatenate([high, low], axis=0), sketch_t_ref[part, :], ((1,), (0,)))
+            total = total + both[:STEP] + both[STEP:]
         flat = total.T
         flat = flat[:48] + flat[48:96]
         for tile in range(STEP // LANES):

time: 88.4 us -> 85.8 us (0.971)
  Pallas kernels: 13.3 us -> 10.7 us
    pallas_call x5, Pallas kernels: 13.3 us -> 10.7 us  [call(): pl.pallas_call(kernel, out_shape=outs, compiler_params=pltpu.CompilerPara...]
where the time goes in v6:
time: 85.8 us; the launch traced here: 85.5 us
  blocking collectives  61.7 us (72%)
  starting transfers between devices  10.8 us (13%)
  Pallas kernels  10.7 us (12%)
  local copies, waits for them, and re-layouts  0.87 us (1%)
    all_to_all x4, blocking collectives, exchange(): return lax.all_to_all(blocks, axis, split_axis=0, concat_axis=0, tiled=True)  61.7 us
    ppermute x1, starting transfers between devices, local(): mine = lax.ppermute(mine, ROW + COL, pairs)  10.8 us
    pallas_call x5, Pallas kernels, call(): pl.pallas_call(kernel, out_shape=outs, compiler_params=pltpu.CompilerPara...  10.7 us
  transfers between devices with their start and end apart: 1, of which 0 were waited for; matrix products, arithmetic and copies ran while one was open for 0% of the time, Pallas kernels for 3%

profile of v6, /device:TPU:8, one launch (start us, length us, event | category | flops | bytes accessed | tf_op | source)
XLA Modules:
  0.0 85.5 jit_solution(7753006481138753301)
XLA Ops:
  0.7 0.9 dynamic_slice.3
  1.6 10.8 %collective-permute-start = (f32[16,1024]{1,0:T(8,128)S(1)}, f32[16,1024]{1,0:T(8,128)S(1)}, u32[]{:S(2)}, u32[]{:S(2)}) collective-permute-start(f32[16,1024]{1,0:T(8,128)S(1)} %dynamic_slice.3), channel_id=1, source_target_pairs={{0,8},{1,36},{2,66},{3,110},{4,157},{5,185},{6,215},{7,243},{8,257... | collective-permute-start | bytes 196616 | tf_op jit(solution)/shard_map/ppermute | solution.py:358
  12.4 2.5 %shard_map.50 = (bf16[208,2048]{1,0:T(8,128)(2,1)S(1)}, bf16[2048,128]{1,0:T(8,128)(2,1)S(1)}, f32[64,128]{1,0:T(8,128)S(1)}, f32[8,128]{1,0:T(8,128)S(1)}, bf16[1024,2048]{1,0:T(8,128)(2,1)S(1)}) custom-call(f32[64,2048]{1,0:T(8,128)} %emb_ref.1, f32[40,2048]{1,0:T(8,128)} %sketch_ref.1, bf16[1024,2048]{1,0:T(8,128)(2,1)} %conf_ref.1), custom_call_target="tpu_custom_call" | custom-call | flops 10000000 | bytes 10653696 | tf_op jit(solution)/shard_map/pallas_call | solution.py:246
  14.9 0.0 collective-permute-done
  14.9 8.4 %all_to_all.20.rows_ref = f32[4,16,1024]{2,1,0:T(8,128)S(1)} all-to-all(f32[4,16,1024]{2,1,0:T(8,128)S(1)} %broadcast_in_dim.3), channel_id=1, replica_groups=mesh['x'=4,'y'=8,'z_high'=4,'z_low'=2,'core'=2] {'z_low','core'}, dimensions={0} | all-to-all | bytes 524288 | tf_op jit(solution)/shard_map/all_to_all | solution.py:327
  23.4 4.6 %shard_map.51 = f32[16,24,128]{2,1,0:T(8,128)S(1)} custom-call(f32[4,16,1024]{2,1,0:T(8,128)S(1)} %all_to_all.20.rows_ref, bf16[1024,2048]{1,0:T(8,128)(2,1)S(1)} %get-tuple-element.31.conf_ref, bf16[208,2048]{1,0:T(8,128)(2,1)S(1)} %get-tuple-element.32.points_ref, bf16[2048,128]{1,0:T(8,128)(2,1)S(1)} %get-tuple-element.33.sketch_t_ref, ...), custom_call_target="tpu_custom_call" | custom-call | flops 2147483648 | bytes 6066176 | tf_op jit(solution)/shard_map/pallas_call | solution.py:246
  28.0 19.0 %all_to_all.21.got_ref = f32[16,24,128]{2,1,0:T(8,128)S(1)} all-to-all(f32[16,24,128]{2,1,0:T(8,128)S(1)} %shard_map.51), channel_id=1, replica_groups=mesh['x'=4,'y'=8,'z_high'=4,'z_low'=2,'core'=2] {'z_high','z_low','core'}, dimensions={0} | all-to-all | bytes 393216 | tf_op jit(solution)/shard_map/all_to_all | solution.py:327
  47.0 0.4 shard_map.52
  47.4 13.0 %all_to_all.22.pieces_ref = f32[16,24,128]{2,1,0:T(8,128)S(1)} all-to-all(f32[16,24,128]{2,1,0:T(8,128)S(1)} %shard_map.52), channel_id=1, replica_groups=mesh['x'=4,'y'=8,'z_high'=4,'z_low'=2,'core'=2] {'z_high','z_low','core'}, dimensions={0} | all-to-all | bytes 393216 | tf_op jit(solution)/shard_map/all_to_all | solution.py:327
  60.4 0.5 shard_map.53
  60.8 21.3 %all_to_all.23.grams_ref = f32[32,8,128]{2,1,0:T(8,128)S(1)} all-to-all(f32[32,8,128]{2,1,0:T(8,128)S(1)} %shard_map.53), channel_id=1, replica_groups=mesh['x'=4,'y'=8,'z_high'=4,'z_low'=2,'core'=2] {'x','y'}, dimensions={0} | all-to-all | bytes 262144 | tf_op jit(solution)/shard_map/all_to_all | solution.py:327
  82.2 2.8 %shard_map.54 = (f32[40,1024]{1,0:T(8,128)}, f32[40,40]{1,0:T(8,128)}, s32[1,1]{1,0:T(1,128)}) custom-call(f32[32,8,128]{2,1,0:T(8,128)S(1)} %all_to_all.23.grams_ref, f32[16,24,128]{2,1,0:T(8,128)S(1)} %all_to_all.22.pieces_ref), custom_call_target="tpu_custom_call" | custom-call | flops 40000000 | bytes 497924 | tf_op jit(solution)/shard_map/pallas_call | solution.py:246
  84.9 0.6 while.11
  (1 shorter events, 0.0 us)
Async XLA Ops:
  1.6 13.3 %collective-permute-start = (f32[16,1024]{1,0:T(8,128)S(1)}, f32[16,1024]{1,0:T(8,128)S(1)}, u32[]{:S(2)}, u32[]{:S(2)}) collective-permute-start(f32[16,1024]{1,0:T(8,128)S(1)} %dynamic_slice.3), channel_id=1, source_target_pairs={{0,8},{1,36},{2,66},{3,110},{4,157},{5,185},{6,215},{7,243},{8,257... | collective-permute-start | bytes 196616 | tf_op jit(solution)/shard_map/ppermute | solution.py:358

commit v7 on v6

--- a/solution.py
+++ b/solution.py
@@ -10,8 +10,7 @@
 from jax.sharding import PartitionSpec as P
 
 HIGHEST_PRECISION = lax.Precision.HIGHEST
-ROW, NEAR = ("x", "y"), ("z_low", "core")
-COL = ("z_high",) + NEAR
+ROW, COL = ("x", "y"), ("z", "core")
 LANES = 128
 HALF = 64
 PACK = 24
@@ -90,7 +89,7 @@
 
 def product_kernel(rows_ref, conf_ref, points_ref, sketch_t_ref, shift_ref, mean_ref, out_ref):
     row_dev, wide = conf_ref.shape
-    emb = rows_ref[...].reshape(HALF, row_dev)
+    emb = rows_ref[...]
     moved = emb - shift_ref[:, :1]
     norms = jnp.sum(moved * moved, axis=0, keepdims=True)
     first, second, third = thirds_of(norms)
@@ -327,13 +326,12 @@
     return lax.all_to_all(blocks, axis, split_axis=0, concat_axis=0, tiled=True)
 
 
-def target_of(x, y, z_high, z_low, core):
-    z = 2 * z_high + z_low
+def target_of(x, y, z, core):
     to_x, to_y = z // 2, 4 * (z % 2) + 2 * core
     to_z = (z + 4 + y - to_y + 8) % 8
     away = (x - to_x + 4) % 4
     half, to_core = away % 2, away // 2
-    return (to_x, to_y + half, to_z // 2, to_z % 2, to_core), half, to_z % 2 * 2 + to_core
+    return (to_x, to_y + half, to_z, to_core), half
 
 
 def flat_index(at, sizes):
@@ -344,23 +342,19 @@
 
 
 def local(embeddings, confidence, sketch):
-    n_row, n_near = lax.axis_size(ROW), lax.axis_size(NEAR)
+    n_row = lax.axis_size(ROW)
     row_dev = confidence.shape[0]
     count = row_dev * n_row
 
-    dims = embeddings.shape[0] // n_near
     sizes = tuple(lax.axis_size(axis) for axis in ROW + COL)
     pairs = []
     for at in itertools.product(*(range(size) for size in sizes)):
         pairs.append((flat_index(at, sizes), flat_index(target_of(*at)[0], sizes)))
-    half, part = target_of(*(lax.axis_index(axis) for axis in ROW + COL))[1:]
-    mine = lax.dynamic_slice(embeddings, (part * dims, half * row_dev), (dims, row_dev))
-    mine = lax.ppermute(mine, ROW + COL, pairs)
-    points, sketch_t, shift, mean, near = columns_side(embeddings, sketch, confidence)
-    mine, mean = lax.optimization_barrier((mine, mean))
-    rows = exchange(jnp.broadcast_to(mine[None], (n_near, dims, row_dev)), NEAR)
-
-    partial_pieces = product_pieces(rows, (points, sketch_t, shift, mean, near))
+    half = target_of(*(lax.axis_index(axis) for axis in ROW + COL))[1]
+    mine = lax.dynamic_slice_in_dim(embeddings, half * row_dev, row_dev, 1)
+    rows = lax.ppermute(mine, ROW + COL, pairs)
+
+    partial_pieces = product_pieces(rows, columns_side(embeddings, sketch, confidence))
     pieces = exchange(piece_sum(exchange(partial_pieces, COL)), COL)
     grams = exchange(gram_tile(pieces, n_row), ROW)
     basis, upper_tri, small = factored(grams, pieces, count)
@@ -376,7 +370,7 @@
 
 
 def solution(mesh):
-    chips = jax.sharding.Mesh(mesh.devices.reshape(4, 8, 4, 2, 2), ROW + COL)
+    chips = jax.sharding.Mesh(mesh.devices.reshape(4, 8, 8, 2), ROW + COL)
     placed = (P(None, COL), P(ROW, COL), P(None, COL))
     return jax.shard_map(
         local, mesh=chips, in_specs=placed, out_specs=(P(None, ROW), P()), check_vma=False

time: 85.8 us -> 88.6 us (1.033)
  waiting for transfers between devices: 0.01 us -> 11.1 us
  blocking collectives: 61.7 us -> 53.5 us
    ppermute x1, waiting for transfers between devices: 0.01 us -> 11.1 us  [local(): rows = lax.ppermute(mine, ROW + COL, pairs)]
    all_to_all x4 -> x3, blocking collectives: 61.7 us -> 53.5 us  [exchange(): return lax.all_to_all(blocks, axis, split_axis=0, concat_axis=0, tiled=True)]
  transfers between devices with their start and end apart: 1 -> 1, of which waited for: 0 -> 1; matrix products, arithmetic and copies ran while one was open for 0% -> 0% of each run, Pallas kernels for 3% -> 3%
where the time goes in v7:
time: 88.6 us; the launch traced here: 88.3 us
  blocking collectives  53.5 us (60%)
  waiting for transfers between devices  11.1 us (13%)
  starting transfers between devices  10.8 us (12%)
  Pallas kernels  10.7 us (12%)
  local copies, waits for them, and re-layouts  0.97 us (1%)
    all_to_all x3, blocking collectives, exchange(): return lax.all_to_all(blocks, axis, split_axis=0, concat_axis=0, tiled=True)  53.5 us
    ppermute x1, waiting for transfers between devices, local(): rows = lax.ppermute(mine, ROW + COL, pairs)  11.1 us
    ppermute x1, starting transfers between devices, local(): rows = lax.ppermute(mine, ROW + COL, pairs)  10.8 us
    pallas_call x5, Pallas kernels, call(): pl.pallas_call(kernel, out_shape=outs, compiler_params=pltpu.CompilerPara...  10.7 us
  transfers between devices with their start and end apart: 1, of which 1 were waited for; matrix products, arithmetic and copies ran while one was open for 0% of the time, Pallas kernels for 3%

profile of v7, /device:TPU:8, one launch (start us, length us, event | category | flops | bytes accessed | tf_op | source)
XLA Modules:
  0.0 88.3 jit_solution(195517178343041065)
XLA Ops:
  0.7 1.0 %constant_dynamic-slice_fusion = f32[64,1024]{1,0:T(8,128)S(1)} fusion(f32[64,2048]{1,0:T(8,128)} %emb_ref.1, s32[]{:T(128)S(6)} %select_n.25), kind=kLoop, calls=%fused_computation.17 | loop fusion | bytes 524292 | tf_op jit(solution)/shard_map/dynamic_slice | solution.py:354
  1.7 10.8 %collective-permute-start = (f32[64,1024]{1,0:T(8,128)S(1)}, f32[64,1024]{1,0:T(8,128)S(1)}, u32[]{:S(2)}, u32[]{:S(2)}) collective-permute-start(f32[64,1024]{1,0:T(8,128)S(1)} %constant_dynamic-slice_fusion), channel_id=1, source_target_pairs={{0,8},{1,36},{2,66},{3,110},{4,157},{5,185},{6,215},{7,243},{8,257... | collective-permute-start | bytes 786440 | tf_op jit(solution)/shard_map/ppermute | solution.py:355
  12.5 2.5 %shard_map.50 = (bf16[208,2048]{1,0:T(8,128)(2,1)S(1)}, bf16[2048,128]{1,0:T(8,128)(2,1)S(1)}, f32[64,128]{1,0:T(8,128)S(1)}, f32[8,128]{1,0:T(8,128)S(1)}, bf16[1024,2048]{1,0:T(8,128)(2,1)S(1)}) custom-call(f32[64,2048]{1,0:T(8,128)} %emb_ref.1, f32[40,2048]{1,0:T(8,128)} %sketch_ref.1, bf16[1024,2048]{1,0:T(8,128)(2,1)} %conf_ref.1), custom_call_target="tpu_custom_call" | custom-call | flops 10000000 | bytes 10653696 | tf_op jit(solution)/shard_map/pallas_call | solution.py:245
  15.0 11.1 %collective-permute-done.rows_ref = f32[64,1024]{1,0:T(8,128)S(1)} collective-permute-done((f32[64,1024]{1,0:T(8,128)S(1)}, f32[64,1024]{1,0:T(8,128)S(1)}, u32[]{:S(2)}, u32[]{:S(2)}) %collective-permute-start) | collective-permute-done | bytes 262176 | tf_op jit(solution)/shard_map/ppermute | solution.py:355
  26.0 4.6 %shard_map.51 = f32[16,24,128]{2,1,0:T(8,128)S(1)} custom-call(f32[64,1024]{1,0:T(8,128)S(1)} %collective-permute-done.rows_ref, bf16[1024,2048]{1,0:T(8,128)(2,1)S(1)} %get-tuple-element.27.conf_ref, bf16[208,2048]{1,0:T(8,128)(2,1)S(1)} %get-tuple-element.28.points_ref, bf16[2048,128]{1,0:T(8,128)(2,1)S(1)} %get-tuple-element.29.sketch_t_ref, ...), custom_call_target="tpu_custom_call" | custom-call | flops 2147483648 | bytes 6066176 | tf_op jit(solution)/shard_map/pallas_call | solution.py:245
  30.6 16.4 %all_to_all.15.got_ref = f32[16,24,128]{2,1,0:T(8,128)S(1)} all-to-all(f32[16,24,128]{2,1,0:T(8,128)S(1)} %shard_map.51), channel_id=1, replica_groups=mesh['x'=4,'y'=8,'z'=8,'core'=2] {'z','core'}, dimensions={0} | all-to-all | bytes 393216 | tf_op jit(solution)/shard_map/all_to_all | solution.py:326
  47.1 0.4 shard_map.52
  47.5 13.0 %all_to_all.16.pieces_ref = f32[16,24,128]{2,1,0:T(8,128)S(1)} all-to-all(f32[16,24,128]{2,1,0:T(8,128)S(1)} %shard_map.52), channel_id=1, replica_groups=mesh['x'=4,'y'=8,'z'=8,'core'=2] {'z','core'}, dimensions={0} | all-to-all | bytes 393216 | tf_op jit(solution)/shard_map/all_to_all | solution.py:326
  60.5 0.5 shard_map.53
  60.9 24.0 %all_to_all.17.grams_ref = f32[32,8,128]{2,1,0:T(8,128)S(1)} all-to-all(f32[32,8,128]{2,1,0:T(8,128)S(1)} %shard_map.53), channel_id=1, replica_groups=mesh['x'=4,'y'=8,'z'=8,'core'=2] {'x','y'}, dimensions={0} | all-to-all | bytes 262144 | tf_op jit(solution)/shard_map/all_to_all | solution.py:326
  85.0 2.8 %shard_map.54 = (f32[40,1024]{1,0:T(8,128)}, f32[40,40]{1,0:T(8,128)}, s32[1,1]{1,0:T(1,128)}) custom-call(f32[32,8,128]{2,1,0:T(8,128)S(1)} %all_to_all.17.grams_ref, f32[16,24,128]{2,1,0:T(8,128)S(1)} %all_to_all.16.pieces_ref), custom_call_target="tpu_custom_call" | custom-call | flops 40000000 | bytes 497924 | tf_op jit(solution)/shard_map/pallas_call | solution.py:245
  87.8 0.6 while.11
Async XLA Ops:
  1.7 24.4 %collective-permute-start = (f32[64,1024]{1,0:T(8,128)S(1)}, f32[64,1024]{1,0:T(8,128)S(1)}, u32[]{:S(2)}, u32[]{:S(2)}) collective-permute-start(f32[64,1024]{1,0:T(8,128)S(1)} %constant_dynamic-slice_fusion), channel_id=1, source_target_pairs={{0,8},{1,36},{2,66},{3,110},{4,157},{5,185},{6,215},{7,243},{8,257... | collective-permute-start | bytes 786440 | tf_op jit(solution)/shard_map/ppermute | solution.py:355

commit v8 on v6

--- a/solution.py
+++ b/solution.py
@@ -101,18 +101,31 @@
     lane, row = lane_of(shape), row_of(shape)
     means = jnp.broadcast_to(pltpu.roll(mean_ref[...], HALF, 1)[:1], shape)
     is_mean = (row == ONES + 1 - PACK) & (lane >= HALF)
-    for begin in range(0, row_dev, STEP):
-        rows = slice(begin, begin + STEP)
-        near = left[:, rows].T.astype(jnp.bfloat16)[:, :208]
-        total = jnp.zeros((STEP, LANES), jnp.float32)
-        for start in range(0, wide, 256):
-            part = slice(start, start + 256)
-            distance = dot(near, points_ref[:, part], ((1,), (0,)))
-            weighted = conf_ref[rows, part].astype(jnp.float32) * distance
+    nears = [left[:, at : at + STEP].T.astype(jnp.bfloat16)[:, :208] for at in range(0, row_dev, STEP)]
+    parts = [slice(start, start + 256) for start in range(0, wide, 256)]
+    tiles = [(step, part) for step in range(row_dev // STEP) for part in parts]
+    totals = [jnp.zeros((STEP, LANES), jnp.float32) for _ in nears]
+
+    def distances(tile):
+        step, part = tile
+        return dot(nears[step], points_ref[:, part], ((1,), (0,)))
+
+    ready, split = distances(tiles[0]), None
+    for at in range(len(tiles) + 1):
+        distance, last = ready, split
+        if at + 1 < len(tiles):
+            ready = distances(tiles[at + 1])
+        if last is not None:
+            step, part = tiles[at - 1]
+            both = dot(last, sketch_t_ref[part, :], ((1,), (0,)))
+            totals[step] = totals[step] + both[:STEP] + both[STEP:]
+        if at < len(tiles):
+            step, part = tiles[at]
+            weighted = conf_ref[step * STEP : (step + 1) * STEP, part].astype(jnp.float32) * distance
             high = weighted.astype(jnp.bfloat16)
             low = (weighted - high.astype(jnp.float32)).astype(jnp.bfloat16)
-            both = dot(jnp.concatenate([high, low], axis=0), sketch_t_ref[part, :], ((1,), (0,)))
-            total = total + both[:STEP] + both[STEP:]
+            split = jnp.concatenate([high, low], axis=0)
+    for step, total in enumerate(totals):
         flat = total.T
         flat = flat[:48] + flat[48:96]
         for tile in range(STEP // LANES):
@@ -120,7 +133,7 @@
             bottom = flat[PACK:, tile * LANES : (tile + 1) * LANES]
             even = jnp.where(lane < HALF, top, pltpu.roll(bottom, HALF, 1))
             odd = jnp.where(lane < HALF, pltpu.roll(top, HALF, 1), bottom)
-            at = begin // HALF + 2 * tile
+            at = step * (STEP // HALF) + 2 * tile
             out_ref[at] = jnp.where(is_mean, means, even)
             out_ref[at + 1] = jnp.where(is_mean, means, odd)
 
@@ -151,8 +164,9 @@
     return jnp.concatenate([jnp.concatenate(tops, axis=1), jnp.concatenate(bottoms, axis=1)], axis=0)
 
 
-def gram_kernel(pieces_ref, out_ref):
+def gram_kernel(pieces_ref, out_ref, product_ref):
     product = unpack(pieces_ref)
+    product_ref[...] = product
     padded = jnp.concatenate([product, jnp.zeros((LANES - 48, product.shape[1]), jnp.float32)], axis=0)
     gram = dot(product, padded, ((1,), (1,)), HIGHEST_PRECISION)
     lane = lane_of((8, LANES))
@@ -173,7 +187,7 @@
     return jnp.broadcast_to(rows[at : at + 1, :], (8, LANES))
 
 
-def factor_kernel(count, grams_ref, pieces_ref, basis_ref, upper_ref, small_ref, basis_near, upper_near, sems):
+def factor_kernel(count, grams_ref, product_ref, basis_ref, upper_ref, small_ref, basis_near, upper_near, sems):
     packed = grams_ref[0]
     for block in range(1, grams_ref.shape[0]):
         packed = packed + grams_ref[block]
@@ -227,7 +241,7 @@
     upper_copy.start()
     solve = jnp.concatenate(scaled, axis=0) * -math.sqrt(count)
     solve = pltpu.roll(solve, LANES - INV, 1)[:, :48]
-    product = unpack(pieces_ref)
+    product = product_ref[...]
     basis_copies = []
     for half in range(2):
         part = pl.ds(half * (product.shape[1] // 2), product.shape[1] // 2)
@@ -300,11 +314,12 @@
 
 
 def gram_tile(pieces, copies):
-    return call(gram_kernel, (array(copies, 8, LANES),), 40_000_000, pieces)[0]
-
-
-def factored(grams, pieces, count):
-    points = pieces.shape[0] * HALF
+    outs = (array(copies, 8, LANES), array(48, pieces.shape[0] * HALF))
+    return call(gram_kernel, outs, 40_000_000, pieces)
+
+
+def factored(grams, product, count):
+    points = product.shape[1]
     outs = (pltpu.HBM((40, points), jnp.float32), pltpu.HBM((40, 40), jnp.float32), array(1, 1, dtype=jnp.int32))
     vmem, smem, hbm = (pl.BlockSpec(memory_space=space) for space in (pltpu.VMEM, pltpu.SMEM, pltpu.HBM))
     return call(
@@ -312,7 +327,7 @@
         outs,
         40_000_000,
         grams,
-        pieces,
+        product,
         in_specs=[vmem, vmem],
         out_specs=(hbm, hbm, smem),
         scratch_shapes=[
@@ -362,8 +377,8 @@
 
     partial_pieces = product_pieces(rows, (points, sketch_t, shift, mean, near))
     pieces = exchange(piece_sum(exchange(partial_pieces, COL)), COL)
-    grams = exchange(gram_tile(pieces, n_row), ROW)
-    basis, upper_tri, small = factored(grams, pieces, count)
+    grams, product = gram_tile(pieces, n_row)
+    basis, upper_tri, small = factored(exchange(grams, ROW), product, count)
 
     def second_pass(state):
         basis, upper_tri, _ = state

time: 85.8 us -> 85.7 us (level)
  no operation moved by 1% of the time
where the time goes in v8:
time: 85.7 us; the launch traced here: 85.3 us
  blocking collectives  61.7 us (72%)
  starting transfers between devices  10.8 us (13%)
  Pallas kernels  10.6 us (12%)
  local copies, waits for them, and re-layouts  0.87 us (1%)
    all_to_all x4, blocking collectives, exchange(): return lax.all_to_all(blocks, axis, split_axis=0, concat_axis=0, tiled=True)  61.7 us
    ppermute x1, starting transfers between devices, local(): mine = lax.ppermute(mine, ROW + COL, pairs)  10.8 us
    pallas_call x5, Pallas kernels, call(): pl.pallas_call(kernel, out_shape=outs, compiler_params=pltpu.CompilerPara...  10.6 us
  transfers between devices with their start and end apart: 1, of which 0 were waited for; matrix products, arithmetic and copies ran while one was open for 0% of the time, Pallas kernels for 3%

profile of v8, /device:TPU:8, one launch (start us, length us, event | category | flops | bytes accessed | tf_op | source)
XLA Modules:
  0.0 85.3 jit_solution(2855516922715802405)
XLA Ops:
  0.7 0.9 dynamic_slice.3
  1.6 10.8 %collective-permute-start = (f32[16,1024]{1,0:T(8,128)S(1)}, f32[16,1024]{1,0:T(8,128)S(1)}, u32[]{:S(2)}, u32[]{:S(2)}) collective-permute-start(f32[16,1024]{1,0:T(8,128)S(1)} %dynamic_slice.3), channel_id=1, source_target_pairs={{0,8},{1,36},{2,66},{3,110},{4,157},{5,185},{6,215},{7,243},{8,257... | collective-permute-start | bytes 196616 | tf_op jit(solution)/shard_map/ppermute | solution.py:373
  12.4 2.5 %shard_map.50 = (bf16[208,2048]{1,0:T(8,128)(2,1)S(1)}, bf16[2048,128]{1,0:T(8,128)(2,1)S(1)}, f32[64,128]{1,0:T(8,128)S(1)}, f32[8,128]{1,0:T(8,128)S(1)}, bf16[1024,2048]{1,0:T(8,128)(2,1)S(1)}) custom-call(f32[64,2048]{1,0:T(8,128)} %emb_ref.1, f32[40,2048]{1,0:T(8,128)} %sketch_ref.1, bf16[1024,2048]{1,0:T(8,128)(2,1)} %conf_ref.1), custom_call_target="tpu_custom_call" | custom-call | flops 10000000 | bytes 10653696 | tf_op jit(solution)/shard_map/pallas_call | solution.py:260
  14.9 0.0 collective-permute-done
  14.9 8.4 %all_to_all.20.rows_ref = f32[4,16,1024]{2,1,0:T(8,128)S(1)} all-to-all(f32[4,16,1024]{2,1,0:T(8,128)S(1)} %broadcast_in_dim.3), channel_id=1, replica_groups=mesh['x'=4,'y'=8,'z_high'=4,'z_low'=2,'core'=2] {'z_low','core'}, dimensions={0} | all-to-all | bytes 524288 | tf_op jit(solution)/shard_map/all_to_all | solution.py:342
  23.4 4.4 %shard_map.51 = f32[16,24,128]{2,1,0:T(8,128)S(1)} custom-call(f32[4,16,1024]{2,1,0:T(8,128)S(1)} %all_to_all.20.rows_ref, bf16[1024,2048]{1,0:T(8,128)(2,1)S(1)} %get-tuple-element.33.conf_ref, bf16[208,2048]{1,0:T(8,128)(2,1)S(1)} %get-tuple-element.34.points_ref, bf16[2048,128]{1,0:T(8,128)(2,1)S(1)} %get-tuple-element.35.sketch_t_ref, ...), custom_call_target="tpu_custom_call" | custom-call | flops 2147483648 | bytes 6066176 | tf_op jit(solution)/shard_map/pallas_call | solution.py:260
  27.8 19.0 %all_to_all.21.got_ref = f32[16,24,128]{2,1,0:T(8,128)S(1)} all-to-all(f32[16,24,128]{2,1,0:T(8,128)S(1)} %shard_map.51), channel_id=1, replica_groups=mesh['x'=4,'y'=8,'z_high'=4,'z_low'=2,'core'=2] {'z_high','z_low','core'}, dimensions={0} | all-to-all | bytes 393216 | tf_op jit(solution)/shard_map/all_to_all | solution.py:342
  46.8 0.4 shard_map.52
  47.2 13.0 %all_to_all.22.pieces_ref = f32[16,24,128]{2,1,0:T(8,128)S(1)} all-to-all(f32[16,24,128]{2,1,0:T(8,128)S(1)} %shard_map.52), channel_id=1, replica_groups=mesh['x'=4,'y'=8,'z_high'=4,'z_low'=2,'core'=2] {'z_high','z_low','core'}, dimensions={0} | all-to-all | bytes 393216 | tf_op jit(solution)/shard_map/all_to_all | solution.py:342
  60.2 0.5 shard_map.53
  60.7 21.3 %all_to_all.23.grams_ref = f32[32,8,128]{2,1,0:T(8,128)S(1)} all-to-all(f32[32,8,128]{2,1,0:T(8,128)S(1)} %get-tuple-element.38), channel_id=1, replica_groups=mesh['x'=4,'y'=8,'z_high'=4,'z_low'=2,'core'=2] {'x','y'}, dimensions={0} | all-to-all | bytes 262144 | tf_op jit(solution)/shard_map/all_to_all | solution.py:342
  82.0 2.8 %shard_map.54 = (f32[40,1024]{1,0:T(8,128)}, f32[40,40]{1,0:T(8,128)}, s32[1,1]{1,0:T(1,128)}) custom-call(f32[32,8,128]{2,1,0:T(8,128)S(1)} %all_to_all.23.grams_ref, f32[48,1024]{1,0:T(8,128)S(1)} %get-tuple-element.39.product_ref), custom_call_target="tpu_custom_call" | custom-call | flops 40000000 | bytes 497924 | tf_op jit(solution)/shard_map/pallas_call | solution.py:260
  84.8 0.6 while.11
  (1 shorter events, 0.0 us)
Async XLA Ops:
  1.6 13.3 %collective-permute-start = (f32[16,1024]{1,0:T(8,128)S(1)}, f32[16,1024]{1,0:T(8,128)S(1)}, u32[]{:S(2)}, u32[]{:S(2)}) collective-permute-start(f32[16,1024]{1,0:T(8,128)S(1)} %dynamic_slice.3), channel_id=1, source_target_pairs={{0,8},{1,36},{2,66},{3,110},{4,157},{5,185},{6,215},{7,243},{8,257... | collective-permute-start | bytes 196616 | tf_op jit(solution)/shard_map/ppermute | solution.py:373

commit v9 on v8

--- a/solution.py
+++ b/solution.py
@@ -239,6 +239,8 @@
         upper_near[base : base + 8, :] = triangle[:, :40]
     upper_copy = pltpu.make_async_copy(upper_near, upper_ref, sems.at[0])
     upper_copy.start()
+    bound = jnp.sum(trace, axis=0, keepdims=True) * jnp.sum(size, axis=0, keepdims=True)
+    small_ref[0, 0] = (bound[0, 0] < 2.5 * 40 * 40).astype(jnp.int32)
     solve = jnp.concatenate(scaled, axis=0) * -math.sqrt(count)
     solve = pltpu.roll(solve, LANES - INV, 1)[:, :48]
     product = product_ref[...]
@@ -249,7 +251,6 @@
         basis_near[:, part] = dot(solve, columns, ((1,), (0,)), HIGHEST_PRECISION)
         basis_copies.append(pltpu.make_async_copy(basis_near.at[:, part], basis_ref.at[:, part], sems.at[1 + half]))
         basis_copies[half].start()
-    small_ref[0, 0] = (jnp.sum(trace) * jnp.sum(size) < 2.5 * 40 * 40).astype(jnp.int32)
     upper_copy.wait()
     for copy in basis_copies:
         copy.wait()

time: 85.7 us -> 85.7 us (level)
  no operation moved by 1% of the time
where the time goes in v9:
time: 85.7 us; the launch traced here: 85.3 us
  blocking collectives  61.7 us (72%)
  starting transfers between devices  10.8 us (13%)
  Pallas kernels  10.6 us (12%)
  local copies, waits for them, and re-layouts  0.87 us (1%)
    all_to_all x4, blocking collectives, exchange(): return lax.all_to_all(blocks, axis, split_axis=0, concat_axis=0, tiled=True)  61.7 us
    ppermute x1, starting transfers between devices, local(): mine = lax.ppermute(mine, ROW + COL, pairs)  10.8 us
    pallas_call x5, Pallas kernels, call(): pl.pallas_call(kernel, out_shape=outs, compiler_params=pltpu.CompilerPara...  10.6 us
  transfers between devices with their start and end apart: 1, of which 0 were waited for; matrix products, arithmetic and copies ran while one was open for 0% of the time, Pallas kernels for 3%

profile of v9, /device:TPU:8, one launch (start us, length us, event | category | flops | bytes accessed | tf_op | source)
XLA Modules:
  0.0 85.3 jit_solution(7479573914394768858)
XLA Ops:
  0.7 0.9 dynamic_slice.3
  1.6 10.8 %collective-permute-start = (f32[16,1024]{1,0:T(8,128)S(1)}, f32[16,1024]{1,0:T(8,128)S(1)}, u32[]{:S(2)}, u32[]{:S(2)}) collective-permute-start(f32[16,1024]{1,0:T(8,128)S(1)} %dynamic_slice.3), channel_id=1, source_target_pairs={{0,8},{1,36},{2,66},{3,110},{4,157},{5,185},{6,215},{7,243},{8,257... | collective-permute-start | bytes 196616 | tf_op jit(solution)/shard_map/ppermute | solution.py:374
  12.4 2.5 %shard_map.50 = (bf16[208,2048]{1,0:T(8,128)(2,1)S(1)}, bf16[2048,128]{1,0:T(8,128)(2,1)S(1)}, f32[64,128]{1,0:T(8,128)S(1)}, f32[8,128]{1,0:T(8,128)S(1)}, bf16[1024,2048]{1,0:T(8,128)(2,1)S(1)}) custom-call(f32[64,2048]{1,0:T(8,128)} %emb_ref.1, f32[40,2048]{1,0:T(8,128)} %sketch_ref.1, bf16[1024,2048]{1,0:T(8,128)(2,1)} %conf_ref.1), custom_call_target="tpu_custom_call" | custom-call | flops 10000000 | bytes 10653696 | tf_op jit(solution)/shard_map/pallas_call | solution.py:261
  14.9 0.0 collective-permute-done
  14.9 8.4 %all_to_all.20.rows_ref = f32[4,16,1024]{2,1,0:T(8,128)S(1)} all-to-all(f32[4,16,1024]{2,1,0:T(8,128)S(1)} %broadcast_in_dim.3), channel_id=1, replica_groups=mesh['x'=4,'y'=8,'z_high'=4,'z_low'=2,'core'=2] {'z_low','core'}, dimensions={0} | all-to-all | bytes 524288 | tf_op jit(solution)/shard_map/all_to_all | solution.py:343
  23.4 4.4 %shard_map.51 = f32[16,24,128]{2,1,0:T(8,128)S(1)} custom-call(f32[4,16,1024]{2,1,0:T(8,128)S(1)} %all_to_all.20.rows_ref, bf16[1024,2048]{1,0:T(8,128)(2,1)S(1)} %get-tuple-element.33.conf_ref, bf16[208,2048]{1,0:T(8,128)(2,1)S(1)} %get-tuple-element.34.points_ref, bf16[2048,128]{1,0:T(8,128)(2,1)S(1)} %get-tuple-element.35.sketch_t_ref, ...), custom_call_target="tpu_custom_call" | custom-call | flops 2147483648 | bytes 6066176 | tf_op jit(solution)/shard_map/pallas_call | solution.py:261
  27.8 19.0 %all_to_all.21.got_ref = f32[16,24,128]{2,1,0:T(8,128)S(1)} all-to-all(f32[16,24,128]{2,1,0:T(8,128)S(1)} %shard_map.51), channel_id=1, replica_groups=mesh['x'=4,'y'=8,'z_high'=4,'z_low'=2,'core'=2] {'z_high','z_low','core'}, dimensions={0} | all-to-all | bytes 393216 | tf_op jit(solution)/shard_map/all_to_all | solution.py:343
  46.8 0.4 shard_map.52
  47.2 13.0 %all_to_all.22.pieces_ref = f32[16,24,128]{2,1,0:T(8,128)S(1)} all-to-all(f32[16,24,128]{2,1,0:T(8,128)S(1)} %shard_map.52), channel_id=1, replica_groups=mesh['x'=4,'y'=8,'z_high'=4,'z_low'=2,'core'=2] {'z_high','z_low','core'}, dimensions={0} | all-to-all | bytes 393216 | tf_op jit(solution)/shard_map/all_to_all | solution.py:343
  60.2 0.5 shard_map.53
  60.7 21.3 %all_to_all.23.grams_ref = f32[32,8,128]{2,1,0:T(8,128)S(1)} all-to-all(f32[32,8,128]{2,1,0:T(8,128)S(1)} %get-tuple-element.38), channel_id=1, replica_groups=mesh['x'=4,'y'=8,'z_high'=4,'z_low'=2,'core'=2] {'x','y'}, dimensions={0} | all-to-all | bytes 262144 | tf_op jit(solution)/shard_map/all_to_all | solution.py:343
  82.0 2.8 %shard_map.54 = (f32[40,1024]{1,0:T(8,128)}, f32[40,40]{1,0:T(8,128)}, s32[1,1]{1,0:T(1,128)}) custom-call(f32[32,8,128]{2,1,0:T(8,128)S(1)} %all_to_all.23.grams_ref, f32[48,1024]{1,0:T(8,128)S(1)} %get-tuple-element.39.product_ref), custom_call_target="tpu_custom_call" | custom-call | flops 40000000 | bytes 497924 | tf_op jit(solution)/shard_map/pallas_call | solution.py:261
  84.8 0.6 while.11
  (1 shorter events, 0.0 us)
Async XLA Ops:
  1.6 13.3 %collective-permute-start = (f32[16,1024]{1,0:T(8,128)S(1)}, f32[16,1024]{1,0:T(8,128)S(1)}, u32[]{:S(2)}, u32[]{:S(2)}) collective-permute-start(f32[16,1024]{1,0:T(8,128)S(1)} %dynamic_slice.3), channel_id=1, source_target_pairs={{0,8},{1,36},{2,66},{3,110},{4,157},{5,185},{6,215},{7,243},{8,257... | collective-permute-start | bytes 196616 | tf_op jit(solution)/shard_map/ppermute | solution.py:374
